TPU v7x, 512 devices: a whole 4x8x8 slice. The times are simulated.
512 devices in a mesh: pair: 128 (over z, x, y_lo, core), dp: 4 (over y_hi).
Axes of the slice: x: 4, y: 8 (y_hi: 4, y_lo: 2; y = y_hi * 2 + y_lo), z: 8, core: 2. Of those that a mesh axis runs over, the one named last changes fastest.
Arguments:
- encoder_activations: bfloat16 [131072, 1024], P(('pair', 'dp')), may hold values from -0.75 to 0.75
- mapping_matrix: bfloat16 [1024, 1024], replicated, may hold values from -0.1875 to 0.1875
- affinity_sharpness: float32 [1], replicated, may hold values from 4 to 8
- affinity_offset: float32 [1], replicated, may hold values from -3 to -1
- segment_number_at_slot: int32 [128], replicated, may hold values from 0 to 127, as said below
- positive_match_targets: int32 [131072], P(('pair', 'dp')), may hold values from 0 to 32767, as said below
Outputs:
- grad_features: bfloat16 [131072, 1024], P(('pair', 'dp'))
- grad_proj: float32 [1024, 1024], P('pair')
Inputs may be any that keep to these rules, and one draw needn't show every extreme that they name: `segment_number_at_slot`: a permutation of the block numbers, the same for every dp index. `positive_match_targets`: the block-row index of the row's positive within its dp group; the relation is mutual and no row is its own positive.
All inputs are finite; a program needn't handle non-finite values.
Results may differ from a plain program's by a relative error of at most 0.0056.
Values may be sent and summed in bfloat16 or wider, within the bound.
A program may use at most 64 MiB of HBM per device.

v0:
```python
import jax
import jax.numpy as jnp
from jax import lax
from jax.sharding import PartitionSpec as P

ROUNDS = 2


epsilon = 1e-06


def partner_2(array, axis, stride):
    return lax.ppermute(array, axis, [(i, i ^ 1 << stride) for i in range(lax.axis_size(axis))])


def embed(row_block, weight):
    projected = jnp.dot(row_block, weight, preferred_element_type=jnp.float32)
    inverse_norm = lax.rsqrt(jnp.sum(projected * projected, axis=-1, keepdims=True) + epsilon)
    return (projected, inverse_norm, (projected * inverse_norm).astype(jnp.bfloat16))


def tile_weight(
    local_rows,
    other_rows,
    other_group_index,
    local_labels,
    smoothing_factor,
    shift_amount,
    group_copies,
    identical_block,
):
    pair_logits = lax.dot_general(
        local_rows, other_rows, (((1,), (1,)), ((), ())), preferred_element_type=jnp.float32
    )
    pair_logits = pair_logits * smoothing_factor + shift_amount
    signs = jnp.where(local_labels[:, None] == other_group_index[None, :], 1.0, -1.0).astype(
        jnp.float32
    )
    pair_coefficient = -signs * jax.nn.sigmoid(-signs * pair_logits) / group_copies
    if identical_block:
        row_ids = lax.broadcasted_iota(jnp.int32, pair_coefficient.shape, 0)
        col_ids = lax.broadcasted_iota(jnp.int32, pair_coefficient.shape, 1)
        pair_coefficient = jnp.where(
            row_ids == col_ids, jnp.zeros_like(pair_coefficient), pair_coefficient
        )
    return (2.0 * smoothing_factor * pair_coefficient).astype(jnp.bfloat16)


def body(
    encoder_activations,
    mapping_matrix,
    affinity_sharpness,
    affinity_offset,
    segment_number_at_slot,
    positive_match_targets,
):
    row_count = encoder_activations.shape[0]
    smoothing_factor = affinity_sharpness[0]
    shift_amount = affinity_offset[0]
    group_copies = lax.axis_size("dp")
    my_index = lax.axis_index("pair")
    row_local = lax.iota(jnp.int32, row_count)
    projected, inverse_norm, embedded_rows = embed(encoder_activations, mapping_matrix)
    own_group_index = segment_number_at_slot[my_index] * row_count + row_local
    self_weight = tile_weight(
        embedded_rows,
        embedded_rows,
        own_group_index,
        positive_match_targets,
        smoothing_factor,
        shift_amount,
        group_copies,
        True,
    )
    grad_embedded = jnp.dot(self_weight, embedded_rows, preferred_element_type=jnp.float32)
    for round_bit in range(ROUNDS):
        partner = jnp.bitwise_xor(my_index, 1 << round_bit)
        other_group_index = segment_number_at_slot[partner] * row_count + row_local
        other_rows = partner_2(embedded_rows, "pair", round_bit)
        pairing_weight = tile_weight(
            embedded_rows,
            other_rows,
            other_group_index,
            positive_match_targets,
            smoothing_factor,
            shift_amount,
            group_copies,
            False,
        )
        grad_embedded = grad_embedded + jnp.dot(
            pairing_weight, other_rows, preferred_element_type=jnp.float32
        )
    inner = jnp.sum(projected * grad_embedded, axis=-1, keepdims=True)
    grad_pre = (inverse_norm * grad_embedded - inverse_norm**3 * inner * projected).astype(
        jnp.bfloat16
    )
    grad_features = lax.dot_general(
        grad_pre, mapping_matrix, (((1,), (1,)), ((), ())), preferred_element_type=jnp.float32
    ).astype(jnp.bfloat16)
    share_rows = mapping_matrix.shape[0] // lax.axis_size("pair")
    full_grad = lax.dot_general(
        encoder_activations, grad_pre, (((0,), (0,)), ((), ())), preferred_element_type=jnp.float32
    )
    summed = lax.psum(full_grad, ("pair", "dp"))
    grad_proj = lax.dynamic_slice_in_dim(summed, my_index * share_rows, share_rows, 0)
    return (grad_features, grad_proj)


def solution(mesh):
    in_specs = (P(("pair", "dp"), None), P(), P(), P(), P(), P(("pair", "dp")))
    out_specs = (P(("pair", "dp"), None), P("pair", None))
    return jax.shard_map(body, mesh=mesh, in_specs=in_specs, out_specs=out_specs, check_vma=False)
```

profile of v0, /device:TPU:24, one launch (start us, length us, event | category | flops | bytes accessed | tf_op | source)
XLA Modules:
  0.0 337.2 jit_solution(14515302760611425263)
XLA Ops:
  7.2 0.0 copy-start
  7.2 0.0 copy-start.4
  7.2 0.0 copy-start.5
  7.2 0.0 all-reduce.2.cloned.1.call-start
  7.2 1.5 copy-done
  8.8 1.8 multiply_reduce_fusion.1
  10.6 0.9 multiply_convert_fusion
  11.5 2.3 collective-permute-start.1
  13.9 1.9 collective-permute-start
  15.8 0.0 copy-done.4
  15.8 0.6 fusion.71
  19.5 0.0 copy-done.5
  19.6 3.3 fusion.29
  22.8 0.0 collective-permute-done
  22.8 3.5 %convolution_add_fusion.1 = f32[256,1024]{1,0:T(8,128)} fusion(f32[256,1024]{1,0:T(8,128)} %fusion.29, bf16[256,1024]{1,0:T(8,128)(2,1)} %collective-permute-done, bf16[256,1024]{1,0:T(8,128)(2,1)} %multiply_convert_fusion, f32[]{:T(128)S(6)} %mul.129, s32[256]{0:T(256)S(1)} %iota_add_fusion.1, f32[]{:T(128)} %bitcast.29, f32[]{:T(128)} %bitcast.26, ...), kind=kOutput, calls=%fused_computation.2 | convolution fusion | flops 269484032 | bytes 3147788 | tf_op jit(solution)/shard_map/dot_general | solution.py:90
  26.3 1.1 collective-permute-done.1
  27.4 3.5 %multiply_reduce_fusion = (f32[256]{0:T(256)S(1)}, f32[256,1024]{1,0:T(8,128)}) fusion(f32[256,1024]{1,0:T(8,128)S(1)} %get-tuple-element.8, f32[256,1024]{1,0:T(8,128)} %convolution_add_fusion.1, bf16[256,1024]{1,0:T(8,128)(2,1)} %collective-permute-done.1, bf16[256,1024]{1,0:T(8,128)(2,1)} %multiply_convert_fusion, s32[256]{0:T(256)S(1)} %iota_add_fusion, ...), kind=kOutput, calls=%fused_computation.38 | convolution fusion | flops 270008064 | bytes 4197388 | tf_op jit(solution)/shard_map/dot_general | solution.py:90
  30.9 0.0 copy-start.3
  30.9 1.5 subtract_convert_fusion
  32.4 0.0 copy-start.1
  32.4 0.8 copy-done.1
  33.2 0.0 copy-done.3
  33.2 2.7 convolution_bitcast_fusion
  35.9 0.0 copy-start.2
  35.9 0.0 all-reduce.2.cloned.1.call-update
  35.9 1.0 copy-done.2
  37.0 1.5 convolution_convert_fusion
  38.5 289.8 %all-reduce.2.cloned.1.call-done = f32[1024,1024]{0,1:T(8,128)} async-done(((f32[1024,1024]{0,1:T(8,128)}), f32[1024,1024]{0,1:T(8,128)}) %all-reduce.2.cloned.1.call-update) | async-done | bytes 4194320 | tf_op jit(solution)/shard_map/psum | solution.py:104
  328.3 1.2 constant_dynamic-slice_fusion
  329.6 0.8 copy.8
  (5 shorter events, 0.0 us)
Async XLA Ops:
  7.2 1.6 copy-start
  7.2 8.7 %copy-start.4 = (s32[128]{0:T(128)S(1)}, s32[128]{0:T(128)}, u32[]{:S(2)}) copy-start(s32[128]{0:T(128)} %param.10) | copy-start | bytes 1540
  7.2 12.4 %copy-start.5 = (s32[256]{0:T(256)S(1)}, s32[256]{0:T(256)}, u32[]{:S(2)}) copy-start(s32[256]{0:T(256)} %param.11) | copy-start | bytes 3076
  7.2 321.1 %all-reduce.2.cloned.1.call-start = ((), (), s32[]{:S(2)}) async-start(), calls=%async_computation | async-start | bytes 8388608 | tf_op jit(solution)/shard_map/psum | solution.py:104
  11.5 15.9 %collective-permute-start.1 = (bf16[256,1024]{1,0:T(8,128)(2,1)}, bf16[256,1024]{1,0:T(8,128)(2,1)}, u32[]{:S(2)}, u32[]{:S(2)}) collective-permute-start(bf16[256,1024]{1,0:T(8,128)(2,1)} %multiply_convert_fusion), channel_id=1, source_target_pairs={{0,8},{4,12},{8,0},{12,4},{16,24},{20,28},{24,16},{28,20},{32,40},... | collective-permute-start | bytes 1572872 | tf_op jit(solution)/shard_map/ppermute | solution.py:13
  13.9 8.9 %collective-permute-start = (bf16[256,1024]{1,0:T(8,128)(2,1)}, bf16[256,1024]{1,0:T(8,128)(2,1)}, u32[]{:S(2)}, u32[]{:S(2)}) collective-permute-start(bf16[256,1024]{1,0:T(8,128)(2,1)} %multiply_convert_fusion), channel_id=1, source_target_pairs={{0,4},{4,0},{8,12},{12,8},{16,20},{20,16},{24,28},{28,24},{32,36},... | collective-permute-start | bytes 1572872 | tf_op jit(solution)/shard_map/ppermute | solution.py:13
  30.9 2.3 copy-start.3
  32.4 0.8 copy-start.1
  35.9 1.0 copy-start.2
Sparse Core Ops, SparseCore 0:
  36.1 292.2 all-reduce.1
where the time goes:
time: 338 us; the launch traced here: 337 us
  waiting for transfers between devices  291 us (86%)
  between operations  17.2 us (5%)
  matrix products  16.4 us (5%)
  local copies, waits for them, and re-layouts  5.97 us (2%)
  starting transfers between devices  4.31 us (1%)
    psum x1, waiting for transfers between devices, body(): summed = lax.psum(full_grad, ('pair', 'dp'))  290 us
    dot_general x2, matrix products, body(): jnp.dot(pairing_weight, other_rows, preferred_element_type=jnp.float32)  7.01 us
  transfers between devices with their start and end apart: 3, of which 2 were waited for; matrix products, arithmetic and copies ran while one was open for 3% of the time, Pallas kernels for 0%

commit v1 on v0

v1 whole, which is shorter than its diff:
```python
import functools

import jax
import jax.numpy as jnp
from jax import lax
from jax.experimental import pallas as pl
from jax.experimental.pallas import tpu as pltpu
from jax.sharding import PartitionSpec as P

EPSILON = 1e-06
NX = 4
CHUNKS = 2
F32 = jnp.float32
BF16 = jnp.bfloat16


def dot_nn(a, b):
    return jnp.dot(a, b, preferred_element_type=F32)


def dot_nt(a, b):
    return lax.dot_general(a, b, (((1,), (1,)), ((), ())), preferred_element_type=F32)


def dot_tn(a, b):
    return lax.dot_general(a, b, (((0,), (0,)), ((), ())), preferred_element_type=F32)


def kernel(
    nz,
    nx,
    groups,
    sharp_ref,
    offset_ref,
    seg_ref,
    lab_hbm,
    feat_hbm,
    map_hbm,
    gf_hbm,
    gp_ref,
    feats,
    labels,
    mapping,
    proj,
    inv,
    emb,
    grad_emb,
    grad_pre,
    turned,
    lhs,
    partial,
    mine,
    core_out,
    core_in,
    x_out,
    x_in,
    z_out,
    z_in,
    y_in,
    gf_vmem,
    local_sem,
    feat_sem,
    emb_sem,
    core_sem,
    x_sem,
    z_sem,
    y_sem,
):
    rows, width = feat_hbm.shape
    half = width // 2
    step = rows // CHUNKS
    pair = lax.axis_index("pair")
    group = lax.axis_index("dp")
    core = pair % 2
    y_lo = (pair // 2) % 2
    x_at = (pair // 4) % nx
    z_at = pair // (4 * nx)
    core_mate = pair + 1 - 2 * core
    y_mate = pair + 2 - 4 * y_lo
    diag_mate = y_mate + 1 - 2 * core
    x_mates = [pair + ((x_at + d) % nx - x_at) * 4 for d in range(1, nx)]
    z_mates = [pair + ((z_at + d) % nz - z_at) * (4 * nx) for d in range(1, nz)]
    y_groups = [(group + d) % groups for d in range(1, groups)]
    to_core, to_y = {"pair": core_mate}, {"pair": y_mate}

    load_feat = pltpu.make_async_copy(feat_hbm, feats.at[0], local_sem.at[0])
    load_map = pltpu.make_async_copy(map_hbm, mapping, local_sem.at[1])
    load_lab = pltpu.make_async_copy(lab_hbm, labels.at[0], local_sem.at[2])
    load_feat.start()
    load_map.start()
    load_lab.start()

    def remote(src, dst, sems, at, device):
        return pltpu.make_async_remote_copy(
            src_ref=src,
            dst_ref=dst,
            send_sem=sems.at[0, at],
            recv_sem=sems.at[1, at],
            device_id=device,
            device_id_type=pl.DeviceIdType.MESH,
        )

    barrier = pltpu.get_barrier_semaphore()
    greeted = [to_core, to_y]
    greeted += [{"pair": mate} for mate in x_mates + z_mates]
    greeted += [{"dp": other} for other in y_groups]
    for device in greeted:
        pl.semaphore_signal(barrier, inc=1, device_id=device, device_id_type=pl.DeviceIdType.MESH)
    pl.semaphore_wait(barrier, len(greeted))

    send_feat = []
    for j in range(CHUNKS):
        part = pl.ds(j * step, step)
        send_feat.append(remote(feat_hbm.at[part], feats.at[1, part], feat_sem, j, to_y))
        send_feat[-1].start()
    send_lab = remote(lab_hbm, labels.at[1], feat_sem, CHUNKS, to_y)
    send_lab.start()

    sharp = sharp_ref[0]
    offset = offset_ref[0]

    def embed(slot, part):
        projected = dot_nn(feats[slot, part], mapping[...])
        norm = lax.rsqrt(jnp.sum(projected * projected, axis=-1, keepdims=True) + EPSILON)
        proj[slot, part] = projected
        inv[slot, part] = norm
        emb[slot, part] = (projected * norm).astype(BF16)

    def turn(slot, part, at):
        flipped = feats[slot, part].T.reshape(turned.shape[:4] + (part.size,))
        turned[:, :, :, :, pl.ds(at, part.size)] = flipped

    def weights(left, right, left_first, right_labels, same):
        logits = dot_nt(left, right) * sharp + offset
        row = lax.broadcasted_iota(jnp.int32, logits.shape, 0)
        hit = jnp.where(right_labels == row + left_first, 1.0, 0.0)
        weight = (2.0 / groups * sharp) * (jax.nn.sigmoid(logits) - hit)
        if same:
            column = lax.broadcasted_iota(jnp.int32, logits.shape, 1)
            weight = jnp.where(row == column, 0.0, weight)
        return weight.astype(BF16)

    whole = pl.ds(0, rows)

    load_feat.wait()
    load_map.wait()
    load_lab.wait()
    embed(0, whole)
    send_own = remote(emb.at[0], emb.at[2], emb_sem, 0, to_core)
    send_own.start()
    turn(0, whole, 0)

    own = emb[0]
    weight = weights(own, own, seg_ref[pair] * rows, labels[0], True)
    grad_emb[0] = dot_nn(weight, own)
    send_own.wait_recv()
    weight = weights(emb[2], own, seg_ref[core_mate] * rows, labels[0], False)
    grad_emb[0] += dot_tn(weight, emb[2])

    send_theirs = []
    for j in range(CHUNKS):
        part = pl.ds(j * step, step)
        send_feat[j].wait_recv()
        embed(1, part)
        send_theirs.append(remote(emb.at[1, part], emb.at[3, part], emb_sem, 1 + j, to_core))
        send_theirs[-1].start()
        weight = weights(
            emb[1, part], emb[0], seg_ref[y_mate] * rows + j * step, labels[0], False
        )
        grad_emb[0] += dot_tn(weight, emb[1, part])
        grad_emb[1, part] = dot_nn(weight, emb[0])
        turn(1, part, rows + j * step)

    def finish(slot):
        grad = grad_emb[slot]
        projected = proj[slot]
        norm = inv[slot]
        inner = jnp.sum(projected * grad, axis=-1, keepdims=True)
        grad_pre[pl.ds(slot * rows, rows)] = (
            norm * grad - norm**3 * inner * projected
        ).astype(BF16)

    send_lab.wait_recv()
    finish(0)
    theirs = emb[1]
    weight = weights(theirs, theirs, seg_ref[y_mate] * rows, labels[1], True)
    grad_emb[1] += dot_nn(weight, theirs)
    for x in range(nx):
        lhs[x] = turned[:, x, y_lo]
    for copy in send_theirs:
        copy.wait_recv()
    weight = weights(emb[3], emb[1], seg_ref[diag_mate] * rows, labels[1], False)
    grad_emb[1] += dot_tn(weight, emb[3])
    finish(1)

    product = dot_nn(lhs[...].reshape(nx * nz * 16, 2 * rows), grad_pre[...])
    partial[...] = product.reshape(nx, nz, 2, 8, width)

    def stacked(block):
        return jnp.concatenate([block[..., :half], block[..., half:]], axis=-2)

    core_out[...] = stacked(partial[:, :, 1 - core]).astype(BF16)
    send_core = remote(core_out, core_in, core_sem, 0, to_core)
    send_core.start()
    mine[...] = stacked(partial[:, :, core])
    send_core.wait_recv()
    total = mine[...] + core_in[...].astype(F32)
    mine[...] = total
    x_out[...] = total.astype(BF16)
    send_x = []
    for d in range(1, nx):
        copy = remote(
            x_out.at[(x_at + d) % nx], x_in.at[d - 1], x_sem, d - 1, {"pair": x_mates[d - 1]}
        )
        copy.start()
        send_x.append(copy)

    gf_vmem[...] = dot_nt(grad_pre[pl.ds(0, rows)], mapping[...]).astype(BF16)
    store_gf = pltpu.make_async_copy(gf_vmem, gf_hbm, local_sem.at[3])
    store_gf.start()

    total = mine[x_at]
    for d in range(1, nx):
        send_x[d - 1].wait_recv()
        total = total + x_in[d - 1].astype(F32)
    mine[0] = total
    z_out[...] = total.astype(BF16)
    send_z = []
    for d in range(1, nz):
        copy = remote(
            z_out.at[(z_at + d) % nz], z_in.at[d - 1], z_sem, d - 1, {"pair": z_mates[d - 1]}
        )
        copy.start()
        send_z.append(copy)
    total = mine[0, z_at]
    for d in range(1, nz):
        send_z[d - 1].wait_recv()
        total = total + z_in[d - 1].astype(F32)
    y_in[group] = total.astype(BF16)
    send_y = []
    for d in range(1, groups):
        copy = remote(y_in.at[group], y_in.at[group], y_sem, d - 1, {"dp": y_groups[d - 1]})
        copy.start()
        send_y.append(copy)
    for copy in send_y:
        copy.wait_recv()
    total = y_in[0].astype(F32)
    for at in range(1, groups):
        total = total + y_in[at].astype(F32)
    gp_ref[...] = jnp.concatenate([total[:8], total[8:]], axis=-1)

    store_gf.wait()
    sent = send_feat + [send_lab, send_own] + send_theirs + [send_core] + send_x + send_z + send_y
    for copy in sent:
        copy.wait_send()


def body(nz, nx, groups, feats, mapping, sharp, offset, segments, targets):
    rows, width = feats.shape
    half = width // 2
    smem = pl.BlockSpec(memory_space=pltpu.SMEM)
    anywhere = pl.BlockSpec(memory_space=pl.ANY)

    def sems(n):
        return pltpu.SemaphoreType.DMA((2, n))

    return pl.pallas_call(
        functools.partial(kernel, nz, nx, groups),
        out_shape=(
            jax.ShapeDtypeStruct((rows, width), BF16),
            jax.ShapeDtypeStruct((8, width), F32),
        ),
        in_specs=[smem, smem, smem, anywhere, anywhere, anywhere],
        out_specs=(anywhere, pl.BlockSpec(memory_space=pltpu.VMEM)),
        scratch_shapes=[
            pltpu.VMEM((2, rows, width), BF16),
            pltpu.VMEM((2, 1, rows), jnp.int32),
            pltpu.VMEM((width, width), BF16),
            pltpu.VMEM((2, rows, width), F32),
            pltpu.VMEM((2, rows, 1), F32),
            pltpu.VMEM((4, rows, width), BF16),
            pltpu.VMEM((2, rows, width), F32),
            pltpu.VMEM((2 * rows, width), BF16),
            pltpu.VMEM((nz, nx, 2, 16, 2 * rows), BF16),
            pltpu.VMEM((nx, nz, 16, 2 * rows), BF16),
            pltpu.VMEM((nx, nz, 2, 8, width), F32),
            pltpu.VMEM((nx, nz, 16, half), F32),
            pltpu.VMEM((nx, nz, 16, half), BF16),
            pltpu.VMEM((nx, nz, 16, half), BF16),
            pltpu.VMEM((nx, nz, 16, half), BF16),
            pltpu.VMEM((nx - 1, nz, 16, half), BF16),
            pltpu.VMEM((nz, 16, half), BF16),
            pltpu.VMEM((nz - 1, 16, half), BF16),
            pltpu.VMEM((groups, 16, half), BF16),
            pltpu.VMEM((rows, width), BF16),
            pltpu.SemaphoreType.DMA((4,)),
            sems(CHUNKS + 1),
            sems(CHUNKS + 1),
            sems(1),
            sems(nx - 1),
            sems(nz - 1),
            sems(groups - 1),
        ],
        compiler_params=pltpu.CompilerParams(
            collective_id=0, has_side_effects=True, vmem_limit_bytes=52 * 1024 * 1024
        ),
        cost_estimate=pl.CostEstimate(
            flops=2 * rows * width * (5 * width + 11 * rows),
            bytes_accessed=8 * rows * width,
            transcendentals=5 * rows * rows,
        ),
        name="contrastive",
    )(sharp, offset, segments, targets.reshape(1, rows), feats, mapping)


def solution(mesh, nx=NX):
    nz = mesh.shape["pair"] // (4 * nx)
    in_specs = (P(("pair", "dp"), None), P(), P(), P(), P(), P(("pair", "dp")))
    out_specs = (P(("pair", "dp"), None), P("pair", None))
    return jax.shard_map(
        functools.partial(body, nz, nx, mesh.shape["dp"]),
        mesh=mesh,
        in_specs=in_specs,
        out_specs=out_specs,
        check_vma=False,
    )
```

time: 338 us -> 58.5 us (0.17)
  the two profiles are of different devices: /device:TPU:24 before, /device:TPU:8 now
where the time goes in v1:
time: 58.5 us; the launch traced here: 58.3 us
  Pallas kernels  52.6 us (90%)
  local copies, waits for them, and re-layouts  3.78 us (6%)
  between operations  1.94 us (3%)
    pallas_call x1, Pallas kernels, body(): pl.pallas_call(functools.partial(kernel, nz, nx, groups), out_shape=(jax....  52.6 us
    unnamed x8, local copies, waits for them, and re-layouts  3.78 us

profile of v1, /device:TPU:8, one launch (start us, length us, event | category | flops | bytes accessed | tf_op | source)
XLA Modules:
  0.0 58.3 jit_solution(6947802557904513084)
XLA Ops:
  1.9 0.0 copy-start
  1.9 1.0 %copy-done = bf16[256,1024]{1,0:T(8,128)(2,1)S(1)} copy-done((bf16[256,1024]{1,0:T(8,128)(2,1)S(1)}, bf16[256,1024]{1,0:T(8,128)(2,1)}, u32[]{:S(2)}) %copy-start) | copy-done | bytes 524312
  3.0 0.0 copy-start.1
  3.0 0.7 %copy-done.1 = s32[256]{0:T(256)S(1)} copy-done((s32[256]{0:T(256)S(1)}, s32[256]{0:T(256)}, u32[]{:S(2)}) %copy-start.1) | copy-done | bytes 1048
  3.6 0.0 copy-start.2
  3.6 0.7 %copy-done.2 = s32[128]{0:T(128)S(1)} copy-done((s32[128]{0:T(128)S(1)}, s32[128]{0:T(128)}, u32[]{:S(2)}) %copy-start.2) | copy-done | bytes 536
  4.3 52.6 %contrastive.1 = (bf16[256,1024]{1,0:T(8,128)(2,1)S(1)}, f32[8,1024]{1,0:T(8,128)S(1)}) custom-call(f32[1]{0:T(128)S(6)} %copy.10.sharp_ref, f32[1]{0:T(128)S(6)} %copy.11.offset_ref, s32[128]{0:T(128)S(1)} %copy-done.2, s32[1,256]{1,0:T(1,128)S(1)} %bitcast.1, bf16[256,1024]{1,0:T(8,128)(2,1)S(1)} %copy-done, bf16[1024,1024]{1,0:T(8,128)(2,1)} %map_hbm.1), custom_call_target="tpu_custom_call" | custom-call | flops 4160749568 | bytes 2097152 | tf_op jit(solution)/shard_map/contrastive/pallas_call | solution.py:267
  56.9 0.8 %copy.12 = bf16[256,1024]{1,0:T(8,128)(2,1)} copy(bf16[256,1024]{1,0:T(8,128)(2,1)S(1)} %get-tuple-element.4) | data formatting | bytes 1048576
  57.7 0.6 %copy.13 = f32[8,1024]{1,0:T(8,128)} copy(f32[8,1024]{1,0:T(8,128)S(1)} %get-tuple-element.5) | data formatting | bytes 65536
Async XLA Ops:
  1.9 1.0 %copy-start = (bf16[256,1024]{1,0:T(8,128)(2,1)S(1)}, bf16[256,1024]{1,0:T(8,128)(2,1)}, u32[]{:S(2)}) copy-start(bf16[256,1024]{1,0:T(8,128)(2,1)} %feat_hbm.1) | copy-start | bytes 1572868
  3.0 0.7 %copy-start.1 = (s32[256]{0:T(256)S(1)}, s32[256]{0:T(256)}, u32[]{:S(2)}) copy-start(s32[256]{0:T(256)} %param.11) | copy-start | bytes 3076
  3.6 0.7 %copy-start.2 = (s32[128]{0:T(128)S(1)}, s32[128]{0:T(128)}, u32[]{:S(2)}) copy-start(s32[128]{0:T(128)} %seg_ref.1) | copy-start | bytes 1540

commit v2 on v1

--- a/solution.py
+++ b/solution.py
@@ -32,12 +32,13 @@
     groups,
     sharp_ref,
     offset_ref,
-    seg_ref,
+    seg_hbm,
     lab_hbm,
     feat_hbm,
     map_hbm,
     gf_hbm,
     gp_ref,
+    seg_ref,
     feats,
     labels,
     mapping,
@@ -54,6 +55,8 @@
     core_in,
     x_out,
     x_in,
+    relay_out,
+    z_sum,
     z_out,
     z_in,
     y_in,
@@ -67,7 +70,7 @@
     y_sem,
 ):
     rows, width = feat_hbm.shape
-    half = width // 2
+    half, quarter = width // 2, width // 4
     step = rows // CHUNKS
     pair = lax.axis_index("pair")
     group = lax.axis_index("dp")
@@ -78,7 +81,8 @@
     core_mate = pair + 1 - 2 * core
     y_mate = pair + 2 - 4 * y_lo
     diag_mate = y_mate + 1 - 2 * core
-    x_mates = [pair + ((x_at + d) % nx - x_at) * 4 for d in range(1, nx)]
+    x_right, x_left, x_far = (x_at + 1) % nx, (x_at + nx - 1) % nx, (x_at + 2) % nx
+    right, left = pair + (x_right - x_at) * 4, pair + (x_left - x_at) * 4
     z_mates = [pair + ((z_at + d) % nz - z_at) * (4 * nx) for d in range(1, nz)]
     y_groups = [(group + d) % groups for d in range(1, groups)]
     to_core, to_y = {"pair": core_mate}, {"pair": y_mate}
@@ -86,9 +90,10 @@
     load_feat = pltpu.make_async_copy(feat_hbm, feats.at[0], local_sem.at[0])
     load_map = pltpu.make_async_copy(map_hbm, mapping, local_sem.at[1])
     load_lab = pltpu.make_async_copy(lab_hbm, labels.at[0], local_sem.at[2])
-    load_feat.start()
-    load_map.start()
-    load_lab.start()
+    load_seg = pltpu.make_async_copy(seg_hbm, seg_ref, local_sem.at[4])
+    loads = [load_feat, load_map, load_lab, load_seg]
+    for copy in loads:
+        copy.start()
 
     def remote(src, dst, sems, at, device):
         return pltpu.make_async_remote_copy(
@@ -102,7 +107,7 @@
 
     barrier = pltpu.get_barrier_semaphore()
     greeted = [to_core, to_y]
-    greeted += [{"pair": mate} for mate in x_mates + z_mates]
+    greeted += [{"pair": mate} for mate in [right, left] + z_mates]
     greeted += [{"dp": other} for other in y_groups]
     for device in greeted:
         pl.semaphore_signal(barrier, inc=1, device_id=device, device_id_type=pl.DeviceIdType.MESH)
@@ -115,9 +120,6 @@
         send_feat[-1].start()
     send_lab = remote(lab_hbm, labels.at[1], feat_sem, CHUNKS, to_y)
     send_lab.start()
-
-    sharp = sharp_ref[0]
-    offset = offset_ref[0]
 
     def embed(slot, part):
         projected = dot_nn(feats[slot, part], mapping[...])
@@ -144,11 +146,15 @@
 
     load_feat.wait()
     load_map.wait()
-    load_lab.wait()
     embed(0, whole)
     send_own = remote(emb.at[0], emb.at[2], emb_sem, 0, to_core)
     send_own.start()
     turn(0, whole, 0)
+
+    for copy in loads[2:]:
+        copy.wait()
+    sharp = sharp_ref[0]
+    offset = offset_ref[0]
 
     own = emb[0]
     weight = weights(own, own, seg_ref[pair] * rows, labels[0], True)
@@ -193,71 +199,110 @@
     grad_emb[1] += dot_tn(weight, emb[3])
     finish(1)
 
-    product = dot_nn(lhs[...].reshape(nx * nz * 16, 2 * rows), grad_pre[...])
-    partial[...] = product.reshape(nx, nz, 2, 8, width)
-
     def stacked(block):
-        return jnp.concatenate([block[..., :half], block[..., half:]], axis=-2)
-
-    core_out[...] = stacked(partial[:, :, 1 - core]).astype(BF16)
-    send_core = remote(core_out, core_in, core_sem, 0, to_core)
-    send_core.start()
-    mine[...] = stacked(partial[:, :, core])
-    send_core.wait_recv()
-    total = mine[...] + core_in[...].astype(F32)
-    mine[...] = total
-    x_out[...] = total.astype(BF16)
-    send_x = []
-    for d in range(1, nx):
-        copy = remote(
-            x_out.at[(x_at + d) % nx], x_in.at[d - 1], x_sem, d - 1, {"pair": x_mates[d - 1]}
-        )
+        return jnp.concatenate([block[..., :quarter], block[..., quarter:]], axis=-2)
+
+    sent = []
+
+    def send(src, dst, sems, at, device):
+        copy = remote(src, dst, sems, at, device)
         copy.start()
-        send_x.append(copy)
+        sent.append(copy)
+        return copy
+
+    left_hand = lhs[...].reshape(nx * nz * 16, 2 * rows)
+    to_right, to_left = {"pair": right}, {"pair": left}
+    core_copies, out_copies, z_copies, y_copies = [], [], [], []
+    for h in range(2):
+        product = dot_nn(left_hand, grad_pre[:, h * half : (h + 1) * half])
+        partial[...] = product.reshape(nx, nz, 2, 8, half)
+        core_out[h] = stacked(partial[:, :, 1 - core]).astype(BF16)
+        core_copies.append(send(core_out.at[h], core_in.at[h], core_sem, h, to_core))
+        mine[h] = stacked(partial[:, :, core])
+
+    lo, hi = pl.ds(0, nz // 2), pl.ds(nz // 2, nz // 2)
+    for h in range(2):
+        core_copies[h].wait_recv()
+        total = mine[h] + core_in[h].astype(F32)
+        mine[h] = total
+        x_out[h] = total.astype(BF16)
+        out_copies.append(
+            [
+                send(x_out.at[h, x_far, lo], x_in.at[h, 0], x_sem, 6 * h, to_right),
+                send(x_out.at[h, x_far, hi], x_in.at[h, 1], x_sem, 6 * h + 1, to_left),
+                send(x_out.at[h, x_right, hi], x_in.at[h, 2], x_sem, 6 * h + 2, to_right),
+                send(x_out.at[h, x_left, lo], x_in.at[h, 3], x_sem, 6 * h + 3, to_left),
+            ]
+        )
+
+    for h in range(2):
+        out_copies[h][0].wait_recv()
+        relay_out[h, 0] = (mine[h, x_right, lo] + x_in[h, 0].astype(F32)).astype(BF16)
+        copies = out_copies[h]
+        copies.append(send(relay_out.at[h, 0], x_in.at[h, 4], x_sem, 6 * h + 4, to_right))
+        copies[1].wait_recv()
+        relay_out[h, 1] = (mine[h, x_left, hi] + x_in[h, 1].astype(F32)).astype(BF16)
+        copies.append(send(relay_out.at[h, 1], x_in.at[h, 5], x_sem, 6 * h + 5, to_left))
 
     gf_vmem[...] = dot_nt(grad_pre[pl.ds(0, rows)], mapping[...]).astype(BF16)
     store_gf = pltpu.make_async_copy(gf_vmem, gf_hbm, local_sem.at[3])
     store_gf.start()
 
-    total = mine[x_at]
-    for d in range(1, nx):
-        send_x[d - 1].wait_recv()
-        total = total + x_in[d - 1].astype(F32)
-    mine[0] = total
-    z_out[...] = total.astype(BF16)
-    send_z = []
-    for d in range(1, nz):
-        copy = remote(
-            z_out.at[(z_at + d) % nz], z_in.at[d - 1], z_sem, d - 1, {"pair": z_mates[d - 1]}
-        )
-        copy.start()
-        send_z.append(copy)
-    total = mine[0, z_at]
-    for d in range(1, nz):
-        send_z[d - 1].wait_recv()
-        total = total + z_in[d - 1].astype(F32)
-    y_in[group] = total.astype(BF16)
-    send_y = []
-    for d in range(1, groups):
-        copy = remote(y_in.at[group], y_in.at[group], y_sem, d - 1, {"dp": y_groups[d - 1]})
-        copy.start()
-        send_y.append(copy)
-    for copy in send_y:
-        copy.wait_recv()
-    total = y_in[0].astype(F32)
-    for at in range(1, groups):
-        total = total + y_in[at].astype(F32)
-    gp_ref[...] = jnp.concatenate([total[:8], total[8:]], axis=-1)
+    for h in range(2):
+        for copy in out_copies[h][2:]:
+            copy.wait_recv()
+        got = [x_in[h, i].astype(F32) for i in range(2, 6)]
+        z_sum[h, lo] = mine[h, x_at, lo] + got[1] + got[2]
+        z_sum[h, hi] = mine[h, x_at, hi] + got[0] + got[3]
+        z_out[h] = z_sum[h].astype(BF16)
+        z_copies.append(
+            [
+                send(
+                    z_out.at[h, (z_at + d) % nz],
+                    z_in.at[h, d - 1],
+                    z_sem,
+                    h * (nz - 1) + d - 1,
+                    {"pair": z_mates[d - 1]},
+                )
+                for d in range(1, nz)
+            ]
+        )
+
+    for h in range(2):
+        total = z_sum[h, z_at]
+        for d in range(1, nz):
+            z_copies[h][d - 1].wait_recv()
+            total = total + z_in[h, d - 1].astype(F32)
+        y_in[h, group] = total.astype(BF16)
+        y_copies.append(
+            [
+                send(
+                    y_in.at[h, group],
+                    y_in.at[h, group],
+                    y_sem,
+                    h * (groups - 1) + d - 1,
+                    {"dp": y_groups[d - 1]},
+                )
+                for d in range(1, groups)
+            ]
+        )
+
+    for h in range(2):
+        for copy in y_copies[h]:
+            copy.wait_recv()
+        total = y_in[h, 0].astype(F32)
+        for at in range(1, groups):
+            total = total + y_in[h, at].astype(F32)
+        gp_ref[:, h * half : (h + 1) * half] = jnp.concatenate([total[:8], total[8:]], axis=-1)
 
     store_gf.wait()
-    sent = send_feat + [send_lab, send_own] + send_theirs + [send_core] + send_x + send_z + send_y
-    for copy in sent:
+    for copy in send_feat + [send_lab, send_own] + send_theirs + sent:
         copy.wait_send()
 
 
 def body(nz, nx, groups, feats, mapping, sharp, offset, segments, targets):
     rows, width = feats.shape
-    half = width // 2
+    half, quarter = width // 2, width // 4
     smem = pl.BlockSpec(memory_space=pltpu.SMEM)
     anywhere = pl.BlockSpec(memory_space=pl.ANY)
 
@@ -270,9 +315,10 @@
             jax.ShapeDtypeStruct((rows, width), BF16),
             jax.ShapeDtypeStruct((8, width), F32),
         ),
-        in_specs=[smem, smem, smem, anywhere, anywhere, anywhere],
+        in_specs=[smem, smem] + [anywhere] * 4,
         out_specs=(anywhere, pl.BlockSpec(memory_space=pltpu.VMEM)),
         scratch_shapes=[
+            pltpu.SMEM(segments.shape, jnp.int32),
             pltpu.VMEM((2, rows, width), BF16),
             pltpu.VMEM((2, 1, rows), jnp.int32),
             pltpu.VMEM((width, width), BF16),
@@ -283,26 +329,28 @@
             pltpu.VMEM((2 * rows, width), BF16),
             pltpu.VMEM((nz, nx, 2, 16, 2 * rows), BF16),
             pltpu.VMEM((nx, nz, 16, 2 * rows), BF16),
-            pltpu.VMEM((nx, nz, 2, 8, width), F32),
-            pltpu.VMEM((nx, nz, 16, half), F32),
-            pltpu.VMEM((nx, nz, 16, half), BF16),
-            pltpu.VMEM((nx, nz, 16, half), BF16),
-            pltpu.VMEM((nx, nz, 16, half), BF16),
-            pltpu.VMEM((nx - 1, nz, 16, half), BF16),
-            pltpu.VMEM((nz, 16, half), BF16),
-            pltpu.VMEM((nz - 1, 16, half), BF16),
-            pltpu.VMEM((groups, 16, half), BF16),
+            pltpu.VMEM((nx, nz, 2, 8, half), F32),
+            pltpu.VMEM((2, nx, nz, 16, quarter), F32),
+            pltpu.VMEM((2, nx, nz, 16, quarter), BF16),
+            pltpu.VMEM((2, nx, nz, 16, quarter), BF16),
+            pltpu.VMEM((2, nx, nz, 16, quarter), BF16),
+            pltpu.VMEM((2, 6, nz // 2, 16, quarter), BF16),
+            pltpu.VMEM((2, 2, nz // 2, 16, quarter), BF16),
+            pltpu.VMEM((2, nz, 16, quarter), F32),
+            pltpu.VMEM((2, nz, 16, quarter), BF16),
+            pltpu.VMEM((2, nz - 1, 16, quarter), BF16),
+            pltpu.VMEM((2, groups, 16, quarter), BF16),
             pltpu.VMEM((rows, width), BF16),
-            pltpu.SemaphoreType.DMA((4,)),
+            pltpu.SemaphoreType.DMA((5,)),
             sems(CHUNKS + 1),
             sems(CHUNKS + 1),
-            sems(1),
-            sems(nx - 1),
-            sems(nz - 1),
-            sems(groups - 1),
+            sems(2),
+            sems(12),
+            sems(2 * (nz - 1)),
+            sems(2 * (groups - 1)),
         ],
         compiler_params=pltpu.CompilerParams(
-            collective_id=0, has_side_effects=True, vmem_limit_bytes=52 * 1024 * 1024
+            collective_id=0, has_side_effects=True, vmem_limit_bytes=63 * 1024 * 1024
         ),
         cost_estimate=pl.CostEstimate(
             flops=2 * rows * width * (5 * width + 11 * rows),

time: 58.5 us -> 55.6 us (0.950)
  Pallas kernels: 52.6 us -> 50.2 us
    pallas_call x1, Pallas kernels: 52.6 us -> 50.2 us  [body(): pl.pallas_call(functools.partial(kernel, nz, nx, groups), out_shape=(jax....]
    unnamed x8 -> x2, local copies, waits for them, and re-layouts: 3.78 us -> 3.24 us
where the time goes in v2:
time: 55.6 us; the launch traced here: 55.4 us
  Pallas kernels  50.2 us (90%)
  local copies, waits for them, and re-layouts  3.24 us (6%)
  between operations  1.93 us (3%)
    pallas_call x1, Pallas kernels, body(): pl.pallas_call(functools.partial(kernel, nz, nx, groups), out_shape=(jax....  50.2 us
    unnamed x2, local copies, waits for them, and re-layouts  3.24 us

profile of v2, /device:TPU:8, one launch (start us, length us, event | category | flops | bytes accessed | tf_op | source)
XLA Modules:
  0.0 55.4 jit_solution(5557225451659899902)
XLA Ops:
  1.9 50.2 %contrastive.1 = (bf16[256,1024]{1,0:T(8,128)(2,1)}, f32[8,1024]{1,0:T(8,128)}) custom-call(f32[1]{0:T(128)S(6)} %copy.10.sharp_ref, f32[1]{0:T(128)S(6)} %copy.11.offset_ref, s32[128]{0:T(128)} %seg_hbm.1, s32[1,256]{1,0:T(1,128)} %bitcast.1, bf16[256,1024]{1,0:T(8,128)(2,1)} %feat_hbm.1, bf16[1024,1024]{1,0:T(8,128)(2,1)} %map_hbm.1), custom_call_target="tpu_custom_call" | custom-call | flops 4160749568 | bytes 2097152 | tf_op jit(solution)/shard_map/contrastive/pallas_call | solution.py:312
  52.1 1.9 %copy.12 = bf16[256,1024]{1,0:T(8,128)(2,1)} copy(bf16[256,1024]{1,0:T(8,128)(2,1)} %get-tuple-element.4) | data formatting | bytes 1048576
  54.0 1.4 %copy.13 = f32[8,1024]{1,0:T(8,128)} copy(f32[8,1024]{1,0:T(8,128)} %get-tuple-element.5) | data formatting | bytes 65536

commit v3 on v2

--- a/solution.py
+++ b/solution.py
@@ -32,8 +32,7 @@
     groups,
     sharp_ref,
     offset_ref,
-    seg_hbm,
-    lab_hbm,
+    int_hbm,
     feat_hbm,
     map_hbm,
     gf_hbm,
@@ -72,6 +71,7 @@
     rows, width = feat_hbm.shape
     half, quarter = width // 2, width // 4
     step = rows // CHUNKS
+    blocks = seg_ref.shape[1]
     pair = lax.axis_index("pair")
     group = lax.axis_index("dp")
     core = pair % 2
@@ -89,8 +89,8 @@
 
     load_feat = pltpu.make_async_copy(feat_hbm, feats.at[0], local_sem.at[0])
     load_map = pltpu.make_async_copy(map_hbm, mapping, local_sem.at[1])
-    load_lab = pltpu.make_async_copy(lab_hbm, labels.at[0], local_sem.at[2])
-    load_seg = pltpu.make_async_copy(seg_hbm, seg_ref, local_sem.at[4])
+    load_lab = pltpu.make_async_copy(int_hbm.at[:, pl.ds(blocks, rows)], labels.at[0], local_sem.at[2])
+    load_seg = pltpu.make_async_copy(int_hbm.at[:, pl.ds(0, blocks)], seg_ref, local_sem.at[4])
     loads = [load_feat, load_map, load_lab, load_seg]
     for copy in loads:
         copy.start()
@@ -113,90 +113,103 @@
         pl.semaphore_signal(barrier, inc=1, device_id=device, device_id_type=pl.DeviceIdType.MESH)
     pl.semaphore_wait(barrier, len(greeted))
 
+    load_feat.wait()
+    load_lab.wait()
+    send_lab = remote(labels.at[0], labels.at[1], feat_sem, CHUNKS, to_y)
+    send_lab.start()
     send_feat = []
     for j in range(CHUNKS):
         part = pl.ds(j * step, step)
-        send_feat.append(remote(feat_hbm.at[part], feats.at[1, part], feat_sem, j, to_y))
+        send_feat.append(remote(feats.at[0, part], feats.at[1, part], feat_sem, j, to_y))
         send_feat[-1].start()
-    send_lab = remote(lab_hbm, labels.at[1], feat_sem, CHUNKS, to_y)
-    send_lab.start()
-
-    def embed(slot, part):
+
+    mate_at, own_at, y_at, diag_at = 0, rows, 2 * rows, 3 * rows
+
+    def embed(slot, start, size):
+        part = pl.ds(start, size)
         projected = dot_nn(feats[slot, part], mapping[...])
         norm = lax.rsqrt(jnp.sum(projected * projected, axis=-1, keepdims=True) + EPSILON)
         proj[slot, part] = projected
         inv[slot, part] = norm
-        emb[slot, part] = (projected * norm).astype(BF16)
-
-    def turn(slot, part, at):
-        flipped = feats[slot, part].T.reshape(turned.shape[:4] + (part.size,))
-        turned[:, :, :, :, pl.ds(at, part.size)] = flipped
-
-    def weights(left, right, left_first, right_labels, same):
+        emb[pl.ds((slot + 1) * rows + start, size)] = (projected * norm).astype(BF16)
+
+    def turn(slot, start, size):
+        flipped = feats[slot, pl.ds(start, size)].T.reshape(turned.shape[:4] + (size,))
+        at = pl.ds(slot * rows + start, size)
+        turned[:, :, :, :, at] = flipped
+        for x in range(nx):
+            lhs[x, :, :, at] = turned[:, x, y_lo, :, at]
+
+    def weights(left_at, left_size, right_at, right_size, right_labels):
+        left = emb[pl.ds(left_at, left_size)]
+        right = emb[pl.ds(right_at, right_size)]
         logits = dot_nt(left, right) * sharp + offset
-        row = lax.broadcasted_iota(jnp.int32, logits.shape, 0)
-        hit = jnp.where(right_labels == row + left_first, 1.0, 0.0)
+        row = lax.broadcasted_iota(jnp.int32, logits.shape, 0) + left_at
+        group_row = row + firsts[left_at // rows]
+        for at in range(left_at // rows + 1, (left_at + left_size - 1) // rows + 1):
+            group_row = jnp.where(row < at * rows, group_row, row + firsts[at])
+        hit = jnp.where(right_labels == group_row, 1.0, 0.0)
         weight = (2.0 / groups * sharp) * (jax.nn.sigmoid(logits) - hit)
-        if same:
-            column = lax.broadcasted_iota(jnp.int32, logits.shape, 1)
+        if left_at < right_at + right_size and right_at < left_at + left_size:
+            column = lax.broadcasted_iota(jnp.int32, logits.shape, 1) + right_at
             weight = jnp.where(row == column, 0.0, weight)
         return weight.astype(BF16)
 
-    whole = pl.ds(0, rows)
-
-    load_feat.wait()
-    load_map.wait()
-    embed(0, whole)
-    send_own = remote(emb.at[0], emb.at[2], emb_sem, 0, to_core)
-    send_own.start()
-    turn(0, whole, 0)
-
-    for copy in loads[2:]:
-        copy.wait()
-    sharp = sharp_ref[0]
-    offset = offset_ref[0]
-
-    own = emb[0]
-    weight = weights(own, own, seg_ref[pair] * rows, labels[0], True)
-    grad_emb[0] = dot_nn(weight, own)
-    send_own.wait_recv()
-    weight = weights(emb[2], own, seg_ref[core_mate] * rows, labels[0], False)
-    grad_emb[0] += dot_tn(weight, emb[2])
-
-    send_theirs = []
-    for j in range(CHUNKS):
-        part = pl.ds(j * step, step)
-        send_feat[j].wait_recv()
-        embed(1, part)
-        send_theirs.append(remote(emb.at[1, part], emb.at[3, part], emb_sem, 1 + j, to_core))
-        send_theirs[-1].start()
-        weight = weights(
-            emb[1, part], emb[0], seg_ref[y_mate] * rows + j * step, labels[0], False
-        )
-        grad_emb[0] += dot_tn(weight, emb[1, part])
-        grad_emb[1, part] = dot_nn(weight, emb[0])
-        turn(1, part, rows + j * step)
-
     def finish(slot):
-        grad = grad_emb[slot]
+        part = pl.ds(slot * rows, rows)
+        grad = grad_emb[part]
         projected = proj[slot]
         norm = inv[slot]
         inner = jnp.sum(projected * grad, axis=-1, keepdims=True)
-        grad_pre[pl.ds(slot * rows, rows)] = (
-            norm * grad - norm**3 * inner * projected
-        ).astype(BF16)
+        grad_pre[part] = (norm * grad - norm**3 * inner * projected).astype(BF16)
+
+    load_map.wait()
+    embed(0, 0, rows)
+    send_own = remote(emb.at[pl.ds(own_at, rows)], emb.at[pl.ds(mate_at, rows)], emb_sem, 0, to_core)
+    send_own.start()
+    load_seg.wait()
+    sharp = sharp_ref[0]
+    offset = offset_ref[0]
+    held = (core_mate, pair, y_mate, diag_mate)
+    firsts = [(seg_ref[0, at] - i) * rows for i, at in enumerate(held)]
+    own_labels = labels[0]
+    turn(0, 0, rows)
+    send_own.wait_recv()
+    weight = weights(mate_at, 2 * rows, own_at, rows, own_labels)
+    grad_emb[pl.ds(0, rows)] = dot_tn(weight, emb[pl.ds(mate_at, 2 * rows)])
+
+    def forward(j):
+        copy = remote(
+            emb.at[pl.ds(y_at + j * step, step)],
+            emb.at[pl.ds(diag_at + j * step, step)],
+            emb_sem,
+            1 + j,
+            to_core,
+        )
+        copy.start()
+        return copy
 
     send_lab.wait_recv()
+    their_labels = labels[1]
+    send_theirs = []
+    for j in range(CHUNKS):
+        at = j * step
+        send_feat[j].wait_recv()
+        embed(1, at, step)
+        send_theirs.append(forward(j))
+        weight = weights(
+            own_at, rows + at + step, y_at + at, step, their_labels[:, at : at + step]
+        )
+        earlier = pl.ds(0, rows + at)
+        theirs = emb[pl.ds(y_at + at, step)]
+        grad_emb[earlier] += dot_nn(weight[: rows + at], theirs)
+        grad_emb[pl.ds(rows + at, step)] = dot_tn(weight, emb[pl.ds(own_at, rows + at + step)])
+        turn(1, at, step)
     finish(0)
-    theirs = emb[1]
-    weight = weights(theirs, theirs, seg_ref[y_mate] * rows, labels[1], True)
-    grad_emb[1] += dot_nn(weight, theirs)
-    for x in range(nx):
-        lhs[x] = turned[:, x, y_lo]
     for copy in send_theirs:
         copy.wait_recv()
-    weight = weights(emb[3], emb[1], seg_ref[diag_mate] * rows, labels[1], False)
-    grad_emb[1] += dot_tn(weight, emb[3])
+    weight = weights(diag_at, rows, y_at, rows, their_labels)
+    grad_emb[pl.ds(rows, rows)] += dot_tn(weight, emb[pl.ds(diag_at, rows)])
     finish(1)
 
     def stacked(block):
@@ -210,6 +223,10 @@
         sent.append(copy)
         return copy
 
+    def features_piece(i):
+        part = pl.ds(i * quarter, quarter)
+        gf_vmem[:, part] = dot_nt(grad_pre[pl.ds(0, rows)], mapping[part]).astype(BF16)
+
     left_hand = lhs[...].reshape(nx * nz * 16, 2 * rows)
     to_right, to_left = {"pair": right}, {"pair": left}
     core_copies, out_copies, z_copies, y_copies = [], [], [], []
@@ -220,6 +237,7 @@
         core_copies.append(send(core_out.at[h], core_in.at[h], core_sem, h, to_core))
         mine[h] = stacked(partial[:, :, core])
 
+    features_piece(0)
     lo, hi = pl.ds(0, nz // 2), pl.ds(nz // 2, nz // 2)
     for h in range(2):
         core_copies[h].wait_recv()
@@ -235,6 +253,7 @@
             ]
         )
 
+    features_piece(1)
     for h in range(2):
         out_copies[h][0].wait_recv()
         relay_out[h, 0] = (mine[h, x_right, lo] + x_in[h, 0].astype(F32)).astype(BF16)
@@ -244,10 +263,7 @@
         relay_out[h, 1] = (mine[h, x_left, hi] + x_in[h, 1].astype(F32)).astype(BF16)
         copies.append(send(relay_out.at[h, 1], x_in.at[h, 5], x_sem, 6 * h + 5, to_left))
 
-    gf_vmem[...] = dot_nt(grad_pre[pl.ds(0, rows)], mapping[...]).astype(BF16)
-    store_gf = pltpu.make_async_copy(gf_vmem, gf_hbm, local_sem.at[3])
-    store_gf.start()
-
+    features_piece(2)
     for h in range(2):
         for copy in out_copies[h][2:]:
             copy.wait_recv()
@@ -268,6 +284,10 @@
             ]
         )
 
+    features_piece(3)
+    store_gf = pltpu.make_async_copy(gf_vmem, gf_hbm, local_sem.at[3])
+    store_gf.start()
+
     for h in range(2):
         total = z_sum[h, z_at]
         for d in range(1, nz):
@@ -306,6 +326,8 @@
     smem = pl.BlockSpec(memory_space=pltpu.SMEM)
     anywhere = pl.BlockSpec(memory_space=pl.ANY)
 
+    integers = jnp.concatenate([segments.reshape(1, -1), targets.reshape(1, -1)], axis=1)
+
     def sems(n):
         return pltpu.SemaphoreType.DMA((2, n))
 
@@ -315,17 +337,17 @@
             jax.ShapeDtypeStruct((rows, width), BF16),
             jax.ShapeDtypeStruct((8, width), F32),
         ),
-        in_specs=[smem, smem] + [anywhere] * 4,
+        in_specs=[smem, smem] + [anywhere] * 3,
         out_specs=(anywhere, pl.BlockSpec(memory_space=pltpu.VMEM)),
         scratch_shapes=[
-            pltpu.SMEM(segments.shape, jnp.int32),
+            pltpu.SMEM((1,) + segments.shape, jnp.int32),
             pltpu.VMEM((2, rows, width), BF16),
             pltpu.VMEM((2, 1, rows), jnp.int32),
             pltpu.VMEM((width, width), BF16),
             pltpu.VMEM((2, rows, width), F32),
             pltpu.VMEM((2, rows, 1), F32),
-            pltpu.VMEM((4, rows, width), BF16),
-            pltpu.VMEM((2, rows, width), F32),
+            pltpu.VMEM((4 * rows, width), BF16),
+            pltpu.VMEM((2 * rows, width), F32),
             pltpu.VMEM((2 * rows, width), BF16),
             pltpu.VMEM((nz, nx, 2, 16, 2 * rows), BF16),
             pltpu.VMEM((nx, nz, 16, 2 * rows), BF16),
@@ -350,7 +372,7 @@
             sems(2 * (groups - 1)),
         ],
         compiler_params=pltpu.CompilerParams(
-            collective_id=0, has_side_effects=True, vmem_limit_bytes=63 * 1024 * 1024
+            collective_id=0, has_side_effects=True, vmem_limit_bytes=53 * 1024 * 1024
         ),
         cost_estimate=pl.CostEstimate(
             flops=2 * rows * width * (5 * width + 11 * rows),
@@ -358,7 +380,7 @@
             transcendentals=5 * rows * rows,
         ),
         name="contrastive",
-    )(sharp, offset, segments, targets.reshape(1, rows), feats, mapping)
+    )(sharp, offset, integers, feats, mapping)
 
 
 def solution(mesh, nx=NX):

time: 55.6 us -> 53.7 us (0.966)
  local copies, waits for them, and re-layouts: 3.24 us -> 1.41 us
  Pallas kernels: 50.2 us -> 49.5 us
  other arithmetic: 0 us -> 0.68 us
    unnamed x2, local copies, waits for them, and re-layouts: 3.24 us -> 1.41 us
    concatenate x0 -> x1, other arithmetic: none -> 0.68 us  [body(): jnp.concatenate([segments.reshape(1, -1), targets.reshape(1, -1)], axis=1)]
    pallas_call x1, Pallas kernels: 50.2 us -> 49.5 us  [body(): pl.pallas_call(functools.partial(kernel, nz, nx, groups), out_shape=(jax....]
where the time goes in v3:
time: 53.7 us; the launch traced here: 53.5 us
  Pallas kernels  49.5 us (92%)
  between operations  1.93 us (4%)
  local copies, waits for them, and re-layouts  1.41 us (3%)
  other arithmetic  0.68 us (1%)
    pallas_call x1, Pallas kernels, body(): pl.pallas_call(functools.partial(kernel, nz, nx, groups), out_shape=(jax....  49.5 us
    unnamed x2, local copies, waits for them, and re-layouts  1.41 us

profile of v3, /device:TPU:8, one launch (start us, length us, event | category | flops | bytes accessed | tf_op | source)
XLA Modules:
  0.0 53.5 jit_solution(13209649697646473911)
XLA Ops:
  1.9 0.7 %pad_add_fusion.int_hbm = s32[1,384]{1,0:T(1,128)S(1)} fusion(s32[1,256]{1,0:T(1,128)} %bitcast.2, s32[1,128]{1,0:T(1,128)} %bitcast.3), kind=kLoop, calls=%fused_computation | loop fusion | flops 384 | bytes 3072 | tf_op jit(solution)/shard_map/concatenate | solution.py:329
  2.6 49.5 %contrastive.1 = (bf16[256,1024]{1,0:T(8,128)(2,1)S(1)}, f32[8,1024]{1,0:T(8,128)S(1)}) custom-call(f32[1]{0:T(128)S(6)} %copy.10.sharp_ref, f32[1]{0:T(128)S(6)} %copy.11.offset_ref, s32[1,384]{1,0:T(1,128)S(1)} %pad_add_fusion.int_hbm, bf16[256,1024]{1,0:T(8,128)(2,1)} %feat_hbm.1, bf16[1024,1024]{1,0:T(8,128)(2,1)} %map_hbm.1), custom_call_target="tpu_custom_call" | custom-call | flops 4160749568 | bytes 2097152 | tf_op jit(solution)/shard_map/contrastive/pallas_call | solution.py:334
  52.1 0.8 %copy.12 = bf16[256,1024]{1,0:T(8,128)(2,1)} copy(bf16[256,1024]{1,0:T(8,128)(2,1)S(1)} %get-tuple-element.4) | data formatting | bytes 1048576
  52.9 0.6 %copy.13 = f32[8,1024]{1,0:T(8,128)} copy(f32[8,1024]{1,0:T(8,128)S(1)} %get-tuple-element.5) | data formatting | bytes 65536

commit v4 on v3

--- a/solution.py
+++ b/solution.py
@@ -48,7 +48,6 @@
     grad_pre,
     turned,
     lhs,
-    partial,
     mine,
     core_out,
     core_in,
@@ -113,14 +112,15 @@
         pl.semaphore_signal(barrier, inc=1, device_id=device, device_id_type=pl.DeviceIdType.MESH)
     pl.semaphore_wait(barrier, len(greeted))
 
-    load_feat.wait()
-    load_lab.wait()
-    send_lab = remote(labels.at[0], labels.at[1], feat_sem, CHUNKS, to_y)
+    send_lab = remote(int_hbm.at[:, pl.ds(blocks, rows)], labels.at[1], feat_sem, CHUNKS, to_y)
     send_lab.start()
+
     send_feat = []
-    for j in range(CHUNKS):
+    for j, source in enumerate((feat_hbm, feats.at[0])):
+        if j > 0:
+            load_feat.wait()
         part = pl.ds(j * step, step)
-        send_feat.append(remote(feats.at[0, part], feats.at[1, part], feat_sem, j, to_y))
+        send_feat.append(remote(source.at[part], feats.at[1, part], feat_sem, j, to_y))
         send_feat[-1].start()
 
     mate_at, own_at, y_at, diag_at = 0, rows, 2 * rows, 3 * rows
@@ -134,11 +134,13 @@
         emb[pl.ds((slot + 1) * rows + start, size)] = (projected * norm).astype(BF16)
 
     def turn(slot, start, size):
-        flipped = feats[slot, pl.ds(start, size)].T.reshape(turned.shape[:4] + (size,))
+        flipped = feats[slot, pl.ds(start, size)].astype(F32).T
         at = pl.ds(slot * rows + start, size)
-        turned[:, :, :, :, at] = flipped
-        for x in range(nx):
-            lhs[x, :, :, at] = turned[:, x, y_lo, :, at]
+        turned[:, :, :, :, :, at] = flipped.reshape(turned.shape[:5] + (size,))
+        for i, owner in enumerate((1 - core, core)):
+            for x in range(nx):
+                block = turned[:, x, y_lo, owner, :, at].reshape(nz * 8, size)
+                lhs[i, pl.ds(x * nz * 8, nz * 8), at] = block.astype(BF16)
 
     def weights(left_at, left_size, right_at, right_size, right_labels):
         left = emb[pl.ds(left_at, left_size)]
@@ -168,6 +170,7 @@
     send_own = remote(emb.at[pl.ds(own_at, rows)], emb.at[pl.ds(mate_at, rows)], emb_sem, 0, to_core)
     send_own.start()
     load_seg.wait()
+    load_lab.wait()
     sharp = sharp_ref[0]
     offset = offset_ref[0]
     held = (core_mate, pair, y_mate, diag_mate)
@@ -212,7 +215,9 @@
     grad_emb[pl.ds(rows, rows)] += dot_tn(weight, emb[pl.ds(diag_at, rows)])
     finish(1)
 
-    def stacked(block):
+    def product(i, h):
+        block = dot_nn(lhs[i], grad_pre[:, h * half : (h + 1) * half])
+        block = block.reshape(nx, nz, 8, half)
         return jnp.concatenate([block[..., :quarter], block[..., quarter:]], axis=-2)
 
     sent = []
@@ -227,42 +232,44 @@
         part = pl.ds(i * quarter, quarter)
         gf_vmem[:, part] = dot_nt(grad_pre[pl.ds(0, rows)], mapping[part]).astype(BF16)
 
-    left_hand = lhs[...].reshape(nx * nz * 16, 2 * rows)
     to_right, to_left = {"pair": right}, {"pair": left}
     core_copies, out_copies, z_copies, y_copies = [], [], [], []
     for h in range(2):
-        product = dot_nn(left_hand, grad_pre[:, h * half : (h + 1) * half])
-        partial[...] = product.reshape(nx, nz, 2, 8, half)
-        core_out[h] = stacked(partial[:, :, 1 - core]).astype(BF16)
+        core_out[h] = product(0, h).astype(BF16)
         core_copies.append(send(core_out.at[h], core_in.at[h], core_sem, h, to_core))
-        mine[h] = stacked(partial[:, :, core])
-
-    features_piece(0)
+    for h in range(2):
+        mine[h] = product(1, h)
+
     lo, hi = pl.ds(0, nz // 2), pl.ds(nz // 2, nz // 2)
-    for h in range(2):
+
+    def send_x(h, i, src):
+        return send(src, x_in.at[h, i], x_sem, 6 * h + i, to_left if i % 2 else to_right)
+
+    def send_far(h):
         core_copies[h].wait_recv()
         total = mine[h] + core_in[h].astype(F32)
         mine[h] = total
         x_out[h] = total.astype(BF16)
-        out_copies.append(
-            [
-                send(x_out.at[h, x_far, lo], x_in.at[h, 0], x_sem, 6 * h, to_right),
-                send(x_out.at[h, x_far, hi], x_in.at[h, 1], x_sem, 6 * h + 1, to_left),
-                send(x_out.at[h, x_right, hi], x_in.at[h, 2], x_sem, 6 * h + 2, to_right),
-                send(x_out.at[h, x_left, lo], x_in.at[h, 3], x_sem, 6 * h + 3, to_left),
-            ]
-        )
-
+        out_copies.append([send_x(h, 0, x_out.at[h, x_far, lo]), send_x(h, 1, x_out.at[h, x_far, hi])])
+
+    def send_direct(h):
+        out_copies[h].append(send_x(h, 2, x_out.at[h, x_right, hi]))
+        out_copies[h].append(send_x(h, 3, x_out.at[h, x_left, lo]))
+
+    def relay(h):
+        for i, (x, part) in enumerate(((x_right, lo), (x_left, hi))):
+            out_copies[h][i].wait_recv()
+            relay_out[h, i] = (mine[h, x, part] + x_in[h, i].astype(F32)).astype(BF16)
+            out_copies[h].append(send_x(h, 4 + i, relay_out.at[h, i]))
+
+    features_piece(0)
+    send_far(0)
+    send_far(1)
+    send_direct(0)
     features_piece(1)
-    for h in range(2):
-        out_copies[h][0].wait_recv()
-        relay_out[h, 0] = (mine[h, x_right, lo] + x_in[h, 0].astype(F32)).astype(BF16)
-        copies = out_copies[h]
-        copies.append(send(relay_out.at[h, 0], x_in.at[h, 4], x_sem, 6 * h + 4, to_right))
-        copies[1].wait_recv()
-        relay_out[h, 1] = (mine[h, x_left, hi] + x_in[h, 1].astype(F32)).astype(BF16)
-        copies.append(send(relay_out.at[h, 1], x_in.at[h, 5], x_sem, 6 * h + 5, to_left))
-
+    relay(0)
+    send_direct(1)
+    relay(1)
     features_piece(2)
     for h in range(2):
         for copy in out_copies[h][2:]:
@@ -349,9 +356,8 @@
             pltpu.VMEM((4 * rows, width), BF16),
             pltpu.VMEM((2 * rows, width), F32),
             pltpu.VMEM((2 * rows, width), BF16),
-            pltpu.VMEM((nz, nx, 2, 16, 2 * rows), BF16),
-            pltpu.VMEM((nx, nz, 16, 2 * rows), BF16),
-            pltpu.VMEM((nx, nz, 2, 8, half), F32),
+            pltpu.VMEM((nz, nx, 2, 2, 8, 2 * rows), F32),
+            pltpu.VMEM((2, nx * nz * 8, 2 * rows), BF16),
             pltpu.VMEM((2, nx, nz, 16, quarter), F32),
             pltpu.VMEM((2, nx, nz, 16, quarter), BF16),
             pltpu.VMEM((2, nx, nz, 16, quarter), BF16),

time: 53.7 us -> 53.3 us (level)
  no operation moved by 1% of the time
where the time goes in v4:
time: 53.3 us; the launch traced here: 53.1 us
  Pallas kernels  49 us (92%)
  between operations  1.93 us (4%)
  local copies, waits for them, and re-layouts  1.41 us (3%)
  other arithmetic  0.68 us (1%)
    pallas_call x1, Pallas kernels, body(): pl.pallas_call(functools.partial(kernel, nz, nx, groups), out_shape=(jax....  49 us
    unnamed x2, local copies, waits for them, and re-layouts  1.41 us

profile of v4, /device:TPU:8, one launch (start us, length us, event | category | flops | bytes accessed | tf_op | source)
XLA Modules:
  0.0 53.1 jit_solution(11094073208497843964)
XLA Ops:
  1.9 0.7 %pad_add_fusion.int_hbm = s32[1,384]{1,0:T(1,128)S(1)} fusion(s32[1,256]{1,0:T(1,128)} %bitcast.2, s32[1,128]{1,0:T(1,128)} %bitcast.3), kind=kLoop, calls=%fused_computation | loop fusion | flops 384 | bytes 3072 | tf_op jit(solution)/shard_map/concatenate | solution.py:336
  2.6 49.0 %contrastive.1 = (bf16[256,1024]{1,0:T(8,128)(2,1)S(1)}, f32[8,1024]{1,0:T(8,128)S(1)}) custom-call(f32[1]{0:T(128)S(6)} %copy.10.sharp_ref, f32[1]{0:T(128)S(6)} %copy.11.offset_ref, s32[1,384]{1,0:T(1,128)S(1)} %pad_add_fusion.int_hbm, bf16[256,1024]{1,0:T(8,128)(2,1)} %feat_hbm.1, bf16[1024,1024]{1,0:T(8,128)(2,1)} %map_hbm.1), custom_call_target="tpu_custom_call" | custom-call | flops 4160749568 | bytes 2097152 | tf_op jit(solution)/shard_map/contrastive/pallas_call | solution.py:341
  51.6 0.8 %copy.12 = bf16[256,1024]{1,0:T(8,128)(2,1)} copy(bf16[256,1024]{1,0:T(8,128)(2,1)S(1)} %get-tuple-element.4) | data formatting | bytes 1048576
  52.4 0.6 %copy.13 = f32[8,1024]{1,0:T(8,128)} copy(f32[8,1024]{1,0:T(8,128)S(1)} %get-tuple-element.5) | data formatting | bytes 65536

commit v5 on v4

--- a/solution.py
+++ b/solution.py
@@ -41,6 +41,7 @@
     feats,
     labels,
     mapping,
+    flipped_map,
     proj,
     inv,
     emb,
@@ -208,6 +209,10 @@
         grad_emb[earlier] += dot_nn(weight[: rows + at], theirs)
         grad_emb[pl.ds(rows + at, step)] = dot_tn(weight, emb[pl.ds(own_at, rows + at + step)])
         turn(1, at, step)
+        if j == 0:
+            for k in range(4):
+                part = pl.ds(k * quarter, quarter)
+                flipped_map[:, part] = mapping[part].T
     finish(0)
     for copy in send_theirs:
         copy.wait_recv()
@@ -227,10 +232,6 @@
         copy.start()
         sent.append(copy)
         return copy
-
-    def features_piece(i):
-        part = pl.ds(i * quarter, quarter)
-        gf_vmem[:, part] = dot_nt(grad_pre[pl.ds(0, rows)], mapping[part]).astype(BF16)
 
     to_right, to_left = {"pair": right}, {"pair": left}
     core_copies, out_copies, z_copies, y_copies = [], [], [], []
@@ -262,15 +263,12 @@
             relay_out[h, i] = (mine[h, x, part] + x_in[h, i].astype(F32)).astype(BF16)
             out_copies[h].append(send_x(h, 4 + i, relay_out.at[h, i]))
 
-    features_piece(0)
     send_far(0)
     send_far(1)
     send_direct(0)
-    features_piece(1)
     relay(0)
     send_direct(1)
     relay(1)
-    features_piece(2)
     for h in range(2):
         for copy in out_copies[h][2:]:
             copy.wait_recv()
@@ -291,10 +289,6 @@
             ]
         )
 
-    features_piece(3)
-    store_gf = pltpu.make_async_copy(gf_vmem, gf_hbm, local_sem.at[3])
-    store_gf.start()
-
     for h in range(2):
         total = z_sum[h, z_at]
         for d in range(1, nz):
@@ -314,6 +308,10 @@
             ]
         )
 
+    gf_vmem[...] = dot_nn(grad_pre[pl.ds(0, rows)], flipped_map[...]).astype(BF16)
+    store_gf = pltpu.make_async_copy(gf_vmem, gf_hbm, local_sem.at[3])
+    store_gf.start()
+
     for h in range(2):
         for copy in y_copies[h]:
             copy.wait_recv()
@@ -350,6 +348,7 @@
             pltpu.SMEM((1,) + segments.shape, jnp.int32),
             pltpu.VMEM((2, rows, width), BF16),
             pltpu.VMEM((2, 1, rows), jnp.int32),
+            pltpu.VMEM((width, width), BF16),
             pltpu.VMEM((width, width), BF16),
             pltpu.VMEM((2, rows, width), F32),
             pltpu.VMEM((2, rows, 1), F32),

time: 53.3 us -> 53.5 us (level)
  no operation moved by 1% of the time
where the time goes in v5:
time: 53.5 us; the launch traced here: 53.3 us
  Pallas kernels  49.3 us (92%)
  between operations  1.93 us (4%)
  local copies, waits for them, and re-layouts  1.41 us (3%)
  other arithmetic  0.68 us (1%)
    pallas_call x1, Pallas kernels, body(): pl.pallas_call(functools.partial(kernel, nz, nx, groups), out_shape=(jax....  49.3 us
    unnamed x2, local copies, waits for them, and re-layouts  1.41 us

profile of v5, /device:TPU:8, one launch (start us, length us, event | category | flops | bytes accessed | tf_op | source)
XLA Modules:
  0.0 53.3 jit_solution(8403307251436871082)
XLA Ops:
  1.9 0.7 %pad_add_fusion.int_hbm = s32[1,384]{1,0:T(1,128)S(1)} fusion(s32[1,256]{1,0:T(1,128)} %bitcast.2, s32[1,128]{1,0:T(1,128)} %bitcast.3), kind=kLoop, calls=%fused_computation | loop fusion | flops 384 | bytes 3072 | tf_op jit(solution)/shard_map/concatenate | solution.py:334
  2.6 49.3 %contrastive.1 = (bf16[256,1024]{1,0:T(8,128)(2,1)S(1)}, f32[8,1024]{1,0:T(8,128)S(1)}) custom-call(f32[1]{0:T(128)S(6)} %copy.10.sharp_ref, f32[1]{0:T(128)S(6)} %copy.11.offset_ref, s32[1,384]{1,0:T(1,128)S(1)} %pad_add_fusion.int_hbm, bf16[256,1024]{1,0:T(8,128)(2,1)} %feat_hbm.1, bf16[1024,1024]{1,0:T(8,128)(2,1)} %map_hbm.1), custom_call_target="tpu_custom_call" | custom-call | flops 4160749568 | bytes 2097152 | tf_op jit(solution)/shard_map/contrastive/pallas_call | solution.py:339
  51.9 0.8 %copy.12 = bf16[256,1024]{1,0:T(8,128)(2,1)} copy(bf16[256,1024]{1,0:T(8,128)(2,1)S(1)} %get-tuple-element.4) | data formatting | bytes 1048576
  52.7 0.6 %copy.13 = f32[8,1024]{1,0:T(8,128)} copy(f32[8,1024]{1,0:T(8,128)S(1)} %get-tuple-element.5) | data formatting | bytes 65536

commit v6 on v5

--- a/solution.py
+++ b/solution.py
@@ -67,6 +67,8 @@
     x_sem,
     z_sem,
     y_sem,
+    z_token,
+    y_token,
 ):
     rows, width = feat_hbm.shape
     half, quarter = width // 2, width // 4
@@ -106,12 +108,32 @@
         )
 
     barrier = pltpu.get_barrier_semaphore()
-    greeted = [to_core, to_y]
-    greeted += [{"pair": mate} for mate in [right, left] + z_mates]
-    greeted += [{"dp": other} for other in y_groups]
+    z_near = [{"pair": z_mates[0]}, {"pair": z_mates[-1]}]
+    greeted = [to_core, to_y, {"pair": right}, {"pair": left}] + z_near
+    greeted += [{"dp": y_groups[0]}, {"dp": y_groups[-1]}]
     for device in greeted:
         pl.semaphore_signal(barrier, inc=1, device_id=device, device_id_type=pl.DeviceIdType.MESH)
     pl.semaphore_wait(barrier, len(greeted))
+
+    def pass_on(i):
+        for side in range(2):
+            pl.semaphore_signal(
+                z_token.at[i, side],
+                inc=1,
+                device_id=z_near[side],
+                device_id_type=pl.DeviceIdType.MESH,
+            )
+
+    def heard(i):
+        for side in range(2):
+            pl.semaphore_wait(z_token.at[i, side], 1)
+
+    tokens = nz // 2 - 1
+    if tokens > 0:
+        pass_on(0)
+    pl.semaphore_signal(
+        y_token, inc=1, device_id={"dp": y_groups[0]}, device_id_type=pl.DeviceIdType.MESH
+    )
 
     send_lab = remote(int_hbm.at[:, pl.ds(blocks, rows)], labels.at[1], feat_sem, CHUNKS, to_y)
     send_lab.start()
@@ -178,6 +200,9 @@
     firsts = [(seg_ref[0, at] - i) * rows for i, at in enumerate(held)]
     own_labels = labels[0]
     turn(0, 0, rows)
+    if tokens > 1:
+        heard(0)
+        pass_on(1)
     send_own.wait_recv()
     weight = weights(mate_at, 2 * rows, own_at, rows, own_labels)
     grad_emb[pl.ds(0, rows)] = dot_tn(weight, emb[pl.ds(mate_at, 2 * rows)])
@@ -210,6 +235,9 @@
         grad_emb[pl.ds(rows + at, step)] = dot_tn(weight, emb[pl.ds(own_at, rows + at + step)])
         turn(1, at, step)
         if j == 0:
+            for i in range(2, tokens):
+                heard(i - 1)
+                pass_on(i)
             for k in range(4):
                 part = pl.ds(k * quarter, quarter)
                 flipped_map[:, part] = mapping[part].T
@@ -269,6 +297,9 @@
     relay(0)
     send_direct(1)
     relay(1)
+    if tokens > 0:
+        heard(tokens - 1)
+    pl.semaphore_wait(y_token, 1)
     for h in range(2):
         for copy in out_copies[h][2:]:
             copy.wait_recv()
@@ -375,6 +406,8 @@
             sems(12),
             sems(2 * (nz - 1)),
             sems(2 * (groups - 1)),
+            pltpu.SemaphoreType.REGULAR((3, 2)),
+            pltpu.SemaphoreType.REGULAR,
         ],
         compiler_params=pltpu.CompilerParams(
             collective_id=0, has_side_effects=True, vmem_limit_bytes=53 * 1024 * 1024

time: 53.5 us -> 52.2 us (0.976)
  Pallas kernels: 49.3 us -> 48 us
    pallas_call x1, Pallas kernels: 49.3 us -> 48 us  [body(): pl.pallas_call(functools.partial(kernel, nz, nx, groups), out_shape=(jax....]
where the time goes in v6:
time: 52.2 us; the launch traced here: 52 us
  Pallas kernels  48 us (92%)
  between operations  1.93 us (4%)
  local copies, waits for them, and re-layouts  1.41 us (3%)
  other arithmetic  0.68 us (1%)
    pallas_call x1, Pallas kernels, body(): pl.pallas_call(functools.partial(kernel, nz, nx, groups), out_shape=(jax....  48 us
    unnamed x2, local copies, waits for them, and re-layouts  1.41 us

profile of v6, /device:TPU:8, one launch (start us, length us, event | category | flops | bytes accessed | tf_op | source)
XLA Modules:
  0.0 52.0 jit_solution(17476865987313709789)
XLA Ops:
  1.9 0.7 %pad_add_fusion.int_hbm = s32[1,384]{1,0:T(1,128)S(1)} fusion(s32[1,256]{1,0:T(1,128)} %bitcast.2, s32[1,128]{1,0:T(1,128)} %bitcast.3), kind=kLoop, calls=%fused_computation | loop fusion | flops 384 | bytes 3072 | tf_op jit(solution)/shard_map/concatenate | solution.py:365
  2.6 48.0 %contrastive.1 = (bf16[256,1024]{1,0:T(8,128)(2,1)S(1)}, f32[8,1024]{1,0:T(8,128)S(1)}) custom-call(f32[1]{0:T(128)S(6)} %copy.10.sharp_ref, f32[1]{0:T(128)S(6)} %copy.11.offset_ref, s32[1,384]{1,0:T(1,128)S(1)} %pad_add_fusion.int_hbm, bf16[256,1024]{1,0:T(8,128)(2,1)} %feat_hbm.1, bf16[1024,1024]{1,0:T(8,128)(2,1)} %map_hbm.1), custom_call_target="tpu_custom_call" | custom-call | flops 4160749568 | bytes 2097152 | tf_op jit(solution)/shard_map/contrastive/pallas_call | solution.py:370
  50.6 0.8 %copy.12 = bf16[256,1024]{1,0:T(8,128)(2,1)} copy(bf16[256,1024]{1,0:T(8,128)(2,1)S(1)} %get-tuple-element.4) | data formatting | bytes 1048576
  51.4 0.6 %copy.13 = f32[8,1024]{1,0:T(8,128)} copy(f32[8,1024]{1,0:T(8,128)S(1)} %get-tuple-element.5) | data formatting | bytes 65536

commit v7 on v6

--- a/solution.py
+++ b/solution.py
@@ -10,6 +10,7 @@
 EPSILON = 1e-06
 NX = 4
 CHUNKS = 2
+PIECES = 2
 F32 = jnp.float32
 BF16 = jnp.bfloat16
 
@@ -72,7 +73,7 @@
 ):
     rows, width = feat_hbm.shape
     half, quarter = width // 2, width // 4
-    step = rows // CHUNKS
+    spans = [(0, rows - rows // 4), (rows - rows // 4, rows // 4)]
     blocks = seg_ref.shape[1]
     pair = lax.axis_index("pair")
     group = lax.axis_index("dp")
@@ -142,7 +143,7 @@
     for j, source in enumerate((feat_hbm, feats.at[0])):
         if j > 0:
             load_feat.wait()
-        part = pl.ds(j * step, step)
+        part = pl.ds(*spans[j])
         send_feat.append(remote(source.at[part], feats.at[1, part], feat_sem, j, to_y))
         send_feat[-1].start()
 
@@ -209,8 +210,8 @@
 
     def forward(j):
         copy = remote(
-            emb.at[pl.ds(y_at + j * step, step)],
-            emb.at[pl.ds(diag_at + j * step, step)],
+            emb.at[pl.ds(y_at + spans[j][0], spans[j][1])],
+            emb.at[pl.ds(diag_at + spans[j][0], spans[j][1])],
             emb_sem,
             1 + j,
             to_core,
@@ -220,20 +221,19 @@
 
     send_lab.wait_recv()
     their_labels = labels[1]
+    all_labels = jnp.concatenate([own_labels, their_labels], axis=1)
     send_theirs = []
-    for j in range(CHUNKS):
-        at = j * step
+    for j, (at, size) in enumerate(spans):
         send_feat[j].wait_recv()
-        embed(1, at, step)
+        embed(1, at, size)
         send_theirs.append(forward(j))
-        weight = weights(
-            own_at, rows + at + step, y_at + at, step, their_labels[:, at : at + step]
-        )
+        width_now = rows + at + size
+        weight = weights(y_at + at, size, own_at, width_now, all_labels[:, :width_now])
         earlier = pl.ds(0, rows + at)
-        theirs = emb[pl.ds(y_at + at, step)]
-        grad_emb[earlier] += dot_nn(weight[: rows + at], theirs)
-        grad_emb[pl.ds(rows + at, step)] = dot_tn(weight, emb[pl.ds(own_at, rows + at + step)])
-        turn(1, at, step)
+        theirs = emb[pl.ds(y_at + at, size)]
+        grad_emb[pl.ds(rows + at, size)] = dot_nn(weight, emb[pl.ds(own_at, width_now)])
+        grad_emb[earlier] += dot_tn(weight[:, : rows + at], theirs)
+        turn(1, j * (rows // 2), rows // 2)
         if j == 0:
             for i in range(2, tokens):
                 heard(i - 1)
@@ -276,10 +276,13 @@
 
     def send_far(h):
         core_copies[h].wait_recv()
-        total = mine[h] + core_in[h].astype(F32)
-        mine[h] = total
-        x_out[h] = total.astype(BF16)
+        total = mine[h, x_far] + core_in[h, x_far].astype(F32)
+        x_out[h, x_far] = total.astype(BF16)
         out_copies.append([send_x(h, 0, x_out.at[h, x_far, lo]), send_x(h, 1, x_out.at[h, x_far, hi])])
+        for x in (x_right, x_left, x_at):
+            total = mine[h, x] + core_in[h, x].astype(F32)
+            mine[h, x] = total
+            x_out[h, x] = total.astype(BF16)
 
     def send_direct(h):
         out_copies[h].append(send_x(h, 2, x_out.at[h, x_right, hi]))
@@ -356,6 +359,18 @@
         copy.wait_send()
 
 
+def hand_over(gf_in, gp_in, gf_out, gp_out, sem):
+    size = gf_in.shape[0] // PIECES
+    copies = [pltpu.make_async_copy(gp_in, gp_out, sem.at[PIECES])]
+    for i in range(PIECES):
+        part = pl.ds(i * size, size)
+        copies.append(pltpu.make_async_copy(gf_in.at[part], gf_out.at[part], sem.at[i]))
+    for copy in copies:
+        copy.start()
+    for copy in copies:
+        copy.wait()
+
+
 def body(nz, nx, groups, feats, mapping, sharp, offset, segments, targets):
     rows, width = feats.shape
     half, quarter = width // 2, width // 4
@@ -367,7 +382,7 @@
     def sems(n):
         return pltpu.SemaphoreType.DMA((2, n))
 
-    return pl.pallas_call(
+    results = pl.pallas_call(
         functools.partial(kernel, nz, nx, groups),
         out_shape=(
             jax.ShapeDtypeStruct((rows, width), BF16),
@@ -419,6 +434,17 @@
         ),
         name="contrastive",
     )(sharp, offset, integers, feats, mapping)
+    return pl.pallas_call(
+        hand_over,
+        out_shape=(
+            jax.ShapeDtypeStruct((rows, width), BF16),
+            jax.ShapeDtypeStruct((8, width), F32),
+        ),
+        in_specs=[pl.BlockSpec(memory_space=pltpu.VMEM)] * 2,
+        out_specs=(anywhere, anywhere),
+        scratch_shapes=[pltpu.SemaphoreType.DMA((PIECES + 1,))],
+        name="hand_over",
+    )(*results)
 
 
 def solution(mesh, nx=NX):

time: 52.2 us -> 54.6 us (1.046)
  Pallas kernels: 48 us -> 50.3 us
    pallas_call x0 -> x1, Pallas kernels: none -> 1.87 us  [body(): pl.pallas_call(hand_over, out_shape=(jax.ShapeDtypeStruct((rows, width),...]
    unnamed x2 -> x4, local copies, waits for them, and re-layouts: 1.41 us -> 1.4 us
where the time goes in v7:
time: 54.6 us; the launch traced here: 54.4 us
  Pallas kernels  50.3 us (92%)
  between operations  1.94 us (4%)
  local copies, waits for them, and re-layouts  1.4 us (3%)
  other arithmetic  0.68 us (1%)
    pallas_call x1, Pallas kernels, body(): pl.pallas_call(functools.partial(kernel, nz, nx, groups), out_shape=(jax....  48.5 us
    pallas_call x1, Pallas kernels, body(): pl.pallas_call(hand_over, out_shape=(jax.ShapeDtypeStruct((rows, width),...  1.87 us
    unnamed x4, local copies, waits for them, and re-layouts  1.4 us

profile of v7, /device:TPU:8, one launch (start us, length us, event | category | flops | bytes accessed | tf_op | source)
XLA Modules:
  0.0 54.4 jit_solution(13116076927849185095)
XLA Ops:
  1.9 0.7 %pad_add_fusion.int_hbm = s32[1,384]{1,0:T(1,128)S(1)} fusion(s32[1,256]{1,0:T(1,128)} %bitcast.2, s32[1,128]{1,0:T(1,128)} %bitcast.3), kind=kLoop, calls=%fused_computation | loop fusion | flops 384 | bytes 3072 | tf_op jit(solution)/shard_map/concatenate | solution.py:380
  2.6 48.5 %contrastive.1 = (bf16[256,1024]{1,0:T(8,128)(2,1)S(1)}, f32[8,1024]{1,0:T(8,128)S(1)}) custom-call(f32[1]{0:T(128)S(6)} %copy.8.sharp_ref, f32[1]{0:T(128)S(6)} %copy.9.offset_ref, s32[1,384]{1,0:T(1,128)S(1)} %pad_add_fusion.int_hbm, bf16[256,1024]{1,0:T(8,128)(2,1)} %feat_hbm.1, bf16[1024,1024]{1,0:T(8,128)(2,1)} %map_hbm.1), custom_call_target="tpu_custom_call" | custom-call | flops 4160749568 | bytes 2097152 | tf_op jit(solution)/shard_map/contrastive/pallas_call | solution.py:385
  51.1 0.0 copy-start
  51.1 0.8 %copy-done = bf16[256,1024]{1,0:T(8,128)(2,1)} copy-done((bf16[256,1024]{1,0:T(8,128)(2,1)}, bf16[256,1024]{1,0:T(8,128)(2,1)S(1)}, u32[]{:S(2)}) %copy-start) | copy-done | bytes 524312
  51.9 0.0 copy-start.1
  51.9 0.6 %copy-done.1 = f32[8,1024]{1,0:T(8,128)} copy-done((f32[8,1024]{1,0:T(8,128)}, f32[8,1024]{1,0:T(8,128)S(1)}, u32[]{:S(2)}) %copy-start.1) | copy-done | bytes 32792
  52.5 1.9 %hand_over.1 = (bf16[256,1024]{1,0:T(8,128)(2,1)}, f32[8,1024]{1,0:T(8,128)}) custom-call(bf16[256,1024]{1,0:T(8,128)(2,1)} %copy-done, f32[8,1024]{1,0:T(8,128)} %copy-done.1), custom_call_target="tpu_custom_call" | custom-call | tf_op jit(solution)/shard_map/hand_over/pallas_call | solution.py:437
Async XLA Ops:
  51.1 0.8 %copy-start = (bf16[256,1024]{1,0:T(8,128)(2,1)}, bf16[256,1024]{1,0:T(8,128)(2,1)S(1)}, u32[]{:S(2)}) copy-start(bf16[256,1024]{1,0:T(8,128)(2,1)S(1)} %get-tuple-element.4.gf_in) | copy-start | bytes 1572868
  51.9 0.6 %copy-start.1 = (f32[8,1024]{1,0:T(8,128)}, f32[8,1024]{1,0:T(8,128)S(1)}, u32[]{:S(2)}) copy-start(f32[8,1024]{1,0:T(8,128)S(1)} %get-tuple-element.5.gp_in) | copy-start | bytes 98308

commit v8 on v6

--- a/solution.py
+++ b/solution.py
@@ -10,6 +10,7 @@
 EPSILON = 1e-06
 NX = 4
 CHUNKS = 2
+PIECES = 2
 F32 = jnp.float32
 BF16 = jnp.bfloat16
 
@@ -53,8 +54,8 @@
     core_out,
     core_in,
     x_out,
+    far_in,
     x_in,
-    relay_out,
     z_sum,
     z_out,
     z_in,
@@ -71,7 +72,8 @@
     y_token,
 ):
     rows, width = feat_hbm.shape
-    half, quarter = width // 2, width // 4
+    half = width // PIECES
+    quarter = half // 2
     step = rows // CHUNKS
     blocks = seg_ref.shape[1]
     pair = lax.axis_index("pair")
@@ -239,7 +241,7 @@
                 heard(i - 1)
                 pass_on(i)
             for k in range(4):
-                part = pl.ds(k * quarter, quarter)
+                part = pl.ds(k * (width // 4), width // 4)
                 flipped_map[:, part] = mapping[part].T
     finish(0)
     for copy in send_theirs:
@@ -263,49 +265,42 @@
 
     to_right, to_left = {"pair": right}, {"pair": left}
     core_copies, out_copies, z_copies, y_copies = [], [], [], []
-    for h in range(2):
+    for h in range(PIECES):
         core_out[h] = product(0, h).astype(BF16)
         core_copies.append(send(core_out.at[h], core_in.at[h], core_sem, h, to_core))
-    for h in range(2):
+    for h in range(PIECES):
         mine[h] = product(1, h)
 
     lo, hi = pl.ds(0, nz // 2), pl.ds(nz // 2, nz // 2)
 
-    def send_x(h, i, src):
-        return send(src, x_in.at[h, i], x_sem, 6 * h + i, to_left if i % 2 else to_right)
+    def send_x(h, i, src, dst):
+        return send(src, dst, x_sem, 4 * h + i, to_left if i % 2 else to_right)
 
     def send_far(h):
         core_copies[h].wait_recv()
         total = mine[h] + core_in[h].astype(F32)
         mine[h] = total
         x_out[h] = total.astype(BF16)
-        out_copies.append([send_x(h, 0, x_out.at[h, x_far, lo]), send_x(h, 1, x_out.at[h, x_far, hi])])
-
-    def send_direct(h):
-        out_copies[h].append(send_x(h, 2, x_out.at[h, x_right, hi]))
-        out_copies[h].append(send_x(h, 3, x_out.at[h, x_left, lo]))
+        out_copies.append(
+            [
+                send_x(h, i, x_out.at[h, x_far, part], far_in.at[h, i])
+                for i, part in enumerate((lo, hi))
+            ]
+        )
 
     def relay(h):
         for i, (x, part) in enumerate(((x_right, lo), (x_left, hi))):
             out_copies[h][i].wait_recv()
-            relay_out[h, i] = (mine[h, x, part] + x_in[h, i].astype(F32)).astype(BF16)
-            out_copies[h].append(send_x(h, 4 + i, relay_out.at[h, i]))
-
-    send_far(0)
-    send_far(1)
-    send_direct(0)
-    relay(0)
-    send_direct(1)
-    relay(1)
-    if tokens > 0:
-        heard(tokens - 1)
-    pl.semaphore_wait(y_token, 1)
-    for h in range(2):
+            x_out[h, x, part] = (mine[h, x, part] + far_in[h, i].astype(F32)).astype(BF16)
+            out_copies[h].append(send_x(h, 2 + i, x_out.at[h, x], x_in.at[h, i]))
+
+    far_first = sorted(range(1, nz), key=lambda d: -min(d, nz - d))
+    far_groups = sorted(range(1, groups), key=lambda d: -min(d, groups - d))
+
+    def send_z(h):
         for copy in out_copies[h][2:]:
             copy.wait_recv()
-        got = [x_in[h, i].astype(F32) for i in range(2, 6)]
-        z_sum[h, lo] = mine[h, x_at, lo] + got[1] + got[2]
-        z_sum[h, hi] = mine[h, x_at, hi] + got[0] + got[3]
+        z_sum[h] = mine[h, x_at] + x_in[h, 0].astype(F32) + x_in[h, 1].astype(F32)
         z_out[h] = z_sum[h].astype(BF16)
         z_copies.append(
             [
@@ -316,14 +311,15 @@
                     h * (nz - 1) + d - 1,
                     {"pair": z_mates[d - 1]},
                 )
-                for d in range(1, nz)
+                for d in far_first
             ]
         )
 
-    for h in range(2):
+    def send_y(h):
+        for copy in z_copies[h]:
+            copy.wait_recv()
         total = z_sum[h, z_at]
         for d in range(1, nz):
-            z_copies[h][d - 1].wait_recv()
             total = total + z_in[h, d - 1].astype(F32)
         y_in[h, group] = total.astype(BF16)
         y_copies.append(
@@ -335,15 +331,30 @@
                     h * (groups - 1) + d - 1,
                     {"dp": y_groups[d - 1]},
                 )
-                for d in range(1, groups)
+                for d in far_groups
             ]
         )
+
+    send_far(0)
+    for h in range(1, PIECES + 1):
+        if h < PIECES:
+            send_far(h)
+        relay(h - 1)
+        if h == 2:
+            if tokens > 0:
+                heard(tokens - 1)
+            pl.semaphore_wait(y_token, 1)
+        if h >= 2:
+            send_z(h - 2)
+    send_z(PIECES - 1)
+    for h in range(PIECES):
+        send_y(h)
 
     gf_vmem[...] = dot_nn(grad_pre[pl.ds(0, rows)], flipped_map[...]).astype(BF16)
     store_gf = pltpu.make_async_copy(gf_vmem, gf_hbm, local_sem.at[3])
     store_gf.start()
 
-    for h in range(2):
+    for h in range(PIECES):
         for copy in y_copies[h]:
             copy.wait_recv()
         total = y_in[h, 0].astype(F32)
@@ -358,7 +369,8 @@
 
 def body(nz, nx, groups, feats, mapping, sharp, offset, segments, targets):
     rows, width = feats.shape
-    half, quarter = width // 2, width // 4
+    half = width // PIECES
+    quarter = half // 2
     smem = pl.BlockSpec(memory_space=pltpu.SMEM)
     anywhere = pl.BlockSpec(memory_space=pl.ANY)
 
@@ -388,24 +400,24 @@
             pltpu.VMEM((2 * rows, width), BF16),
             pltpu.VMEM((nz, nx, 2, 2, 8, 2 * rows), F32),
             pltpu.VMEM((2, nx * nz * 8, 2 * rows), BF16),
-            pltpu.VMEM((2, nx, nz, 16, quarter), F32),
-            pltpu.VMEM((2, nx, nz, 16, quarter), BF16),
-            pltpu.VMEM((2, nx, nz, 16, quarter), BF16),
-            pltpu.VMEM((2, nx, nz, 16, quarter), BF16),
-            pltpu.VMEM((2, 6, nz // 2, 16, quarter), BF16),
-            pltpu.VMEM((2, 2, nz // 2, 16, quarter), BF16),
-            pltpu.VMEM((2, nz, 16, quarter), F32),
-            pltpu.VMEM((2, nz, 16, quarter), BF16),
-            pltpu.VMEM((2, nz - 1, 16, quarter), BF16),
-            pltpu.VMEM((2, groups, 16, quarter), BF16),
+            pltpu.VMEM((PIECES, nx, nz, 16, quarter), F32),
+            pltpu.VMEM((PIECES, nx, nz, 16, quarter), BF16),
+            pltpu.VMEM((PIECES, nx, nz, 16, quarter), BF16),
+            pltpu.VMEM((PIECES, nx, nz, 16, quarter), BF16),
+            pltpu.VMEM((PIECES, 2, nz // 2, 16, quarter), BF16),
+            pltpu.VMEM((PIECES, 2, nz, 16, quarter), BF16),
+            pltpu.VMEM((PIECES, nz, 16, quarter), F32),
+            pltpu.VMEM((PIECES, nz, 16, quarter), BF16),
+            pltpu.VMEM((PIECES, nz - 1, 16, quarter), BF16),
+            pltpu.VMEM((PIECES, groups, 16, quarter), BF16),
             pltpu.VMEM((rows, width), BF16),
             pltpu.SemaphoreType.DMA((5,)),
             sems(CHUNKS + 1),
             sems(CHUNKS + 1),
-            sems(2),
-            sems(12),
-            sems(2 * (nz - 1)),
-            sems(2 * (groups - 1)),
+            sems(PIECES),
+            sems(4 * PIECES),
+            sems(PIECES * (nz - 1)),
+            sems(PIECES * (groups - 1)),
             pltpu.SemaphoreType.REGULAR((3, 2)),
             pltpu.SemaphoreType.REGULAR,
         ],

time: 52.2 us -> 52.2 us (level)
  no operation moved by 1% of the time
where the time goes in v8:
time: 52.2 us; the launch traced here: 52 us
  Pallas kernels  48 us (92%)
  between operations  1.93 us (4%)
  local copies, waits for them, and re-layouts  1.41 us (3%)
  other arithmetic  0.68 us (1%)
    pallas_call x1, Pallas kernels, body(): pl.pallas_call(functools.partial(kernel, nz, nx, groups), out_shape=(jax....  48 us
    unnamed x2, local copies, waits for them, and re-layouts  1.41 us

profile of v8, /device:TPU:8, one launch (start us, length us, event | category | flops | bytes accessed | tf_op | source)
XLA Modules:
  0.0 52.0 jit_solution(13204079617477825288)
XLA Ops:
  1.9 0.7 %pad_add_fusion.int_hbm = s32[1,384]{1,0:T(1,128)S(1)} fusion(s32[1,256]{1,0:T(1,128)} %bitcast.2, s32[1,128]{1,0:T(1,128)} %bitcast.3), kind=kLoop, calls=%fused_computation | loop fusion | flops 384 | bytes 3072 | tf_op jit(solution)/shard_map/concatenate | solution.py:377
  2.6 48.0 %contrastive.1 = (bf16[256,1024]{1,0:T(8,128)(2,1)S(1)}, f32[8,1024]{1,0:T(8,128)S(1)}) custom-call(f32[1]{0:T(128)S(6)} %copy.10.sharp_ref, f32[1]{0:T(128)S(6)} %copy.11.offset_ref, s32[1,384]{1,0:T(1,128)S(1)} %pad_add_fusion.int_hbm, bf16[256,1024]{1,0:T(8,128)(2,1)} %feat_hbm.1, bf16[1024,1024]{1,0:T(8,128)(2,1)} %map_hbm.1), custom_call_target="tpu_custom_call" | custom-call | flops 4160749568 | bytes 2097152 | tf_op jit(solution)/shard_map/contrastive/pallas_call | solution.py:382
  50.6 0.8 %copy.12 = bf16[256,1024]{1,0:T(8,128)(2,1)} copy(bf16[256,1024]{1,0:T(8,128)(2,1)S(1)} %get-tuple-element.4) | data formatting | bytes 1048576
  51.4 0.6 %copy.13 = f32[8,1024]{1,0:T(8,128)} copy(f32[8,1024]{1,0:T(8,128)S(1)} %get-tuple-element.5) | data formatting | bytes 65536

commit v9 on v8

--- a/solution.py
+++ b/solution.py
@@ -297,70 +297,49 @@
     far_first = sorted(range(1, nz), key=lambda d: -min(d, nz - d))
     far_groups = sorted(range(1, groups), key=lambda d: -min(d, groups - d))
 
-    def send_z(h):
+    def sum_x(h):
         for copy in out_copies[h][2:]:
             copy.wait_recv()
-        z_sum[h] = mine[h, x_at] + x_in[h, 0].astype(F32) + x_in[h, 1].astype(F32)
-        z_out[h] = z_sum[h].astype(BF16)
-        z_copies.append(
-            [
-                send(
-                    z_out.at[h, (z_at + d) % nz],
-                    z_in.at[h, d - 1],
-                    z_sem,
-                    h * (nz - 1) + d - 1,
-                    {"pair": z_mates[d - 1]},
-                )
-                for d in far_first
-            ]
-        )
-
-    def send_y(h):
-        for copy in z_copies[h]:
-            copy.wait_recv()
-        total = z_sum[h, z_at]
-        for d in range(1, nz):
-            total = total + z_in[h, d - 1].astype(F32)
-        y_in[h, group] = total.astype(BF16)
-        y_copies.append(
-            [
-                send(
-                    y_in.at[h, group],
-                    y_in.at[h, group],
-                    y_sem,
-                    h * (groups - 1) + d - 1,
-                    {"dp": y_groups[d - 1]},
-                )
-                for d in far_groups
-            ]
-        )
+        total = mine[h, x_at] + x_in[h, 0].astype(F32) + x_in[h, 1].astype(F32)
+        z_sum[:, h] = total
+        z_out[:, h] = total.astype(BF16)
 
     send_far(0)
     for h in range(1, PIECES + 1):
         if h < PIECES:
             send_far(h)
         relay(h - 1)
-        if h == 2:
-            if tokens > 0:
-                heard(tokens - 1)
-            pl.semaphore_wait(y_token, 1)
-        if h >= 2:
-            send_z(h - 2)
-    send_z(PIECES - 1)
     for h in range(PIECES):
-        send_y(h)
+        sum_x(h)
+    if tokens > 0:
+        heard(tokens - 1)
+    pl.semaphore_wait(y_token, 1)
+    for d in far_first:
+        to_mate = {"pair": z_mates[d - 1]}
+        z_copies.append(send(z_out.at[(z_at + d) % nz], z_in.at[d - 1], z_sem, d - 1, to_mate))
+    for copy in z_copies:
+        copy.wait_recv()
+    total = z_sum[z_at]
+    for d in range(1, nz):
+        total = total + z_in[d - 1].astype(F32)
+    y_in[group] = total.astype(BF16)
+    for d in far_groups:
+        to_group = {"dp": y_groups[d - 1]}
+        y_copies.append(send(y_in.at[group], y_in.at[group], y_sem, d - 1, to_group))
 
     gf_vmem[...] = dot_nn(grad_pre[pl.ds(0, rows)], flipped_map[...]).astype(BF16)
     store_gf = pltpu.make_async_copy(gf_vmem, gf_hbm, local_sem.at[3])
     store_gf.start()
 
+    for copy in y_copies:
+        copy.wait_recv()
+    total = y_in[0].astype(F32)
+    for at in range(1, groups):
+        total = total + y_in[at].astype(F32)
     for h in range(PIECES):
-        for copy in y_copies[h]:
-            copy.wait_recv()
-        total = y_in[h, 0].astype(F32)
-        for at in range(1, groups):
-            total = total + y_in[h, at].astype(F32)
-        gp_ref[:, h * half : (h + 1) * half] = jnp.concatenate([total[:8], total[8:]], axis=-1)
+        gp_ref[:, h * half : (h + 1) * half] = jnp.concatenate(
+            [total[h, :8], total[h, 8:]], axis=-1
+        )
 
     store_gf.wait()
     for copy in send_feat + [send_lab, send_own] + send_theirs + sent:
@@ -406,18 +385,18 @@
             pltpu.VMEM((PIECES, nx, nz, 16, quarter), BF16),
             pltpu.VMEM((PIECES, 2, nz // 2, 16, quarter), BF16),
             pltpu.VMEM((PIECES, 2, nz, 16, quarter), BF16),
-            pltpu.VMEM((PIECES, nz, 16, quarter), F32),
-            pltpu.VMEM((PIECES, nz, 16, quarter), BF16),
-            pltpu.VMEM((PIECES, nz - 1, 16, quarter), BF16),
-            pltpu.VMEM((PIECES, groups, 16, quarter), BF16),
+            pltpu.VMEM((nz, PIECES, 16, quarter), F32),
+            pltpu.VMEM((nz, PIECES, 16, quarter), BF16),
+            pltpu.VMEM((nz - 1, PIECES, 16, quarter), BF16),
+            pltpu.VMEM((groups, PIECES, 16, quarter), BF16),
             pltpu.VMEM((rows, width), BF16),
             pltpu.SemaphoreType.DMA((5,)),
             sems(CHUNKS + 1),
             sems(CHUNKS + 1),
             sems(PIECES),
             sems(4 * PIECES),
-            sems(PIECES * (nz - 1)),
-            sems(PIECES * (groups - 1)),
+            sems(nz - 1),
+            sems(groups - 1),
             pltpu.SemaphoreType.REGULAR((3, 2)),
             pltpu.SemaphoreType.REGULAR,
         ],

time: 52.2 us -> 52.9 us (1.013)
  Pallas kernels: 48 us -> 48.7 us
    pallas_call x1, Pallas kernels: 48 us -> 48.7 us  [body(): pl.pallas_call(functools.partial(kernel, nz, nx, groups), out_shape=(jax....]
where the time goes in v9:
time: 52.9 us; the launch traced here: 52.7 us
  Pallas kernels  48.7 us (92%)
  between operations  1.93 us (4%)
  local copies, waits for them, and re-layouts  1.41 us (3%)
  other arithmetic  0.68 us (1%)
    pallas_call x1, Pallas kernels, body(): pl.pallas_call(functools.partial(kernel, nz, nx, groups), out_shape=(jax....  48.7 us
    unnamed x2, local copies, waits for them, and re-layouts  1.41 us

profile of v9, /device:TPU:8, one launch (start us, length us, event | category | flops | bytes accessed | tf_op | source)
XLA Modules:
  0.0 52.7 jit_solution(5585470143374405980)
XLA Ops:
  1.9 0.7 %pad_add_fusion.int_hbm = s32[1,384]{1,0:T(1,128)S(1)} fusion(s32[1,256]{1,0:T(1,128)} %bitcast.2, s32[1,128]{1,0:T(1,128)} %bitcast.3), kind=kLoop, calls=%fused_computation | loop fusion | flops 384 | bytes 3072 | tf_op jit(solution)/shard_map/concatenate | solution.py:356
  2.6 48.7 %contrastive.1 = (bf16[256,1024]{1,0:T(8,128)(2,1)S(1)}, f32[8,1024]{1,0:T(8,128)S(1)}) custom-call(f32[1]{0:T(128)S(6)} %copy.10.sharp_ref, f32[1]{0:T(128)S(6)} %copy.11.offset_ref, s32[1,384]{1,0:T(1,128)S(1)} %pad_add_fusion.int_hbm, bf16[256,1024]{1,0:T(8,128)(2,1)} %feat_hbm.1, bf16[1024,1024]{1,0:T(8,128)(2,1)} %map_hbm.1), custom_call_target="tpu_custom_call" | custom-call | flops 4160749568 | bytes 2097152 | tf_op jit(solution)/shard_map/contrastive/pallas_call | solution.py:361
  51.3 0.8 %copy.12 = bf16[256,1024]{1,0:T(8,128)(2,1)} copy(bf16[256,1024]{1,0:T(8,128)(2,1)S(1)} %get-tuple-element.4) | data formatting | bytes 1048576
  52.1 0.6 %copy.13 = f32[8,1024]{1,0:T(8,128)} copy(f32[8,1024]{1,0:T(8,128)S(1)} %get-tuple-element.5) | data formatting | bytes 65536
